TPU v7x, 32 devices: a whole 2x2x4 slice. The times are simulated.
32 devices in a mesh: row: 2 (over x), col: 16 (over z, y, core).
Axes of the slice: x: 2, y: 2, z: 4, core: 2. Of those that a mesh axis runs over, the one named last changes fastest.
Arguments:
- symmetric: float32 [12288, 12288], P('row', 'col'), may hold values from -24 to 24, as said below
Outputs:
- reduced: float32 [12288, 12288], P('row', 'col')
Inputs may be any that keep to these rules, and one draw needn't show every extreme that they name: symmetric equals its transpose.
All inputs are finite; a program needn't handle non-finite values.
Results may differ from a plain program's by a relative error of at most 0.0001.
Values sent between devices are 32-bit elements; how exact they have to be, the bound alone decides.
A program may use at most 128 MiB of HBM per device.

v0:
```python
import math

import jax
import jax.numpy as jnp
from jax import lax
from jax.sharding import PartitionSpec as P

N = 12288
B = 256


HIGH = lax.Precision.HIGHEST


def from_root(value, axis, source):
    kept = jnp.where(lax.axis_index(axis) == source, value, 0).astype(value.dtype)
    return lax.psum(kept, axis)


def contract(left_op, right_op, left_dim, right_dim):
    return lax.dot_general(
        left_op,
        right_op,
        (((left_dim,), (right_dim,)), ((), ())),
        precision=HIGH,
        preferred_element_type=jnp.float32,
    )


def per_device(symmetric):
    current = symmetric
    rows_dev, cols_dev = current.shape
    row_at = lax.axis_index("row")
    col_at = lax.axis_index("col")
    global_rows = row_at * rows_dev + jnp.arange(rows_dev, dtype=jnp.int32)
    global_cols = col_at * cols_dev + jnp.arange(cols_dev, dtype=jnp.int32)
    band_index = jnp.arange(B, dtype=jnp.int32)
    identity = jnp.eye(B, dtype=jnp.float32)
    which = 0
    first_col = which * B
    below = first_col + B
    column_strip = from_root(current[:, first_col : first_col + B], "col", 0)
    panel_cols = jnp.where((global_rows >= below)[:, None], column_strip, jnp.float32(0.0))
    row_strip = from_root(current[first_col : first_col + B, :], "row", 0)
    panel_trans = jnp.where((global_cols >= below)[None, :], row_strip, jnp.float32(0.0))
    gram_part = contract(panel_cols, panel_cols, 0, 0)
    leading_part = jnp.where(row_at == 0, panel_cols[below : below + B], jnp.float32(0.0))
    gram, leading_rows = lax.psum((gram_part, leading_part), "row")
    lower_factor = jnp.linalg.cholesky(gram)
    basis_rows = lax.linalg.triangular_solve(
        lower_factor, panel_cols, left_side=False, lower=True, transpose_a=True
    )
    leading = lax.linalg.triangular_solve(
        lower_factor, leading_rows, left_side=False, lower=True, transpose_a=True
    )
    row_unit = (global_rows[:, None] - below == band_index[None, :]).astype(jnp.float32)
    reflector = basis_rows - row_unit
    col_unit = (band_index[:, None] == global_cols[None, :] - below).astype(jnp.float32)
    reflector_t = (
        lax.linalg.triangular_solve(lower_factor, panel_trans, left_side=True, lower=True)
        - col_unit
    )
    shifted = identity - leading
    normal_mat = contract(shifted, shifted, 0, 0)
    normal_chol = jnp.linalg.cholesky(normal_mat)
    interim = lax.linalg.triangular_solve(normal_chol, shifted.T, left_side=True, lower=True)
    t_mat = lax.linalg.triangular_solve(
        normal_chol, interim, left_side=True, lower=True, transpose_a=True
    )
    u_row = lax.psum(contract(current, reflector_t, 1, 1), "col")
    core_sum = lax.psum(contract(reflector, u_row, 0, 0), "row")
    middle = contract(contract(t_mat, core_sum, 1, 0), t_mat, 1, 1)
    w_row = contract(u_row, t_mat, 1, 1) - 0.5 * contract(reflector, middle, 1, 0)
    ut_col = lax.psum(contract(reflector, current, 0, 0), "row")
    wt_col = contract(t_mat, ut_col, 1, 0) - 0.5 * contract(middle, reflector_t, 0, 0)
    first_term = contract(reflector, wt_col, 1, 0)
    second_term = contract(w_row, reflector_t, 1, 0)
    current = current - first_term - second_term
    factors = [lower_factor]
    inverse_root = jnp.float32(1.0 / math.sqrt(N))
    which = 0
    first_col = which * B
    below = first_col + B
    r_mat = factors[which].T * inverse_root
    old_strip = current[:, first_col : first_col + B]
    placed = jnp.zeros((rows_dev, B), jnp.float32).at[below : below + B].set(r_mat)
    inside = global_rows[:, None] < below + B
    updated = jnp.where(
        global_rows[:, None] >= below, jnp.where(inside, placed, jnp.float32(0.0)), old_strip
    )
    updated = jnp.where(col_at == 0, updated, old_strip)
    current = current.at[:, first_col : first_col + B].set(updated)
    old_top = current[first_col : first_col + B, :]
    onehot = (global_cols[:, None] - below == band_index[None, :]).astype(jnp.float32)
    mirror = contract(r_mat, onehot, 0, 1)
    new_top = jnp.where((global_cols >= below)[None, :], mirror, old_top)
    new_top = jnp.where(row_at == 0, new_top, old_top)
    current = current.at[first_col : first_col + B, :].set(new_top)
    return current


def solution(mesh):
    in_specs = (P("row", "col"),)
    out_specs = P("row", "col")
    return jax.shard_map(
        per_device, mesh=mesh, in_specs=in_specs, out_specs=out_specs, check_vma=False
    )
```

profile of v0, /device:TPU:0, one launch (start us, length us, event | category | flops | bytes accessed | tf_op | source)
XLA Modules:
  0.0 724.7 jit_solution(1528522493668512387)
XLA Ops:
  6.5 18.6 %copy.19 = f32[6144,768]{0,1:T(8,128)} copy(f32[6144,768]{1,0:T(8,128)} %param.8) | data formatting | bytes 37748736 | tf_op args[0]
  25.2 6.1 slice_select_fusion
  31.4 2.1 slice_select_fusion.1
  33.5 139.7 %all-reduce.9.cloned.1.call-done = f32[6144,256]{0,1:T(8,128)} async-done(((f32[6144,256]{0,1:T(8,128)}), f32[6144,256]{0,1:T(8,128)}) %all-reduce.9.cloned.1.call-update) | async-done | bytes 6291472 | tf_op jit(solution)/shard_map/psum | solution.py:17
  173.2 3.2 broadcast_select_fusion
  176.4 2.7 copy-done
  179.1 5.9 fusion.69
  185.3 40.2 %all-reduce.15.cloned.1.call-done = (f32[256,256]{0,1:T(8,128)}, f32[256,768]{0,1:T(8,128)}) async-done(((f32[256,256]{0,1:T(8,128)}, f32[256,768]{0,1:T(8,128)}), (f32[256,256]{0,1:T(8,128)}, f32[256,768]{0,1:T(8,128)})) %all-reduce.15.cloned.1.call-update) | async-done | bytes 1048592 | tf_op jit(solution)/shard_map/psum | solution.py:48
  225.5 1.1 copy.15
  226.6 1.0 fusion.14
  227.6 11.7 %cholesky.130 = f32[128,128]{1,0:T(8,128)S(1)} custom-call(f32[128,128]{1,0:T(8,128)S(1)} %cholesky.194), custom_call_target="Cholesky" | custom-call | tf_op jit(solution)/shard_map/jit(cholesky)/cholesky | solution.py:49
  239.3 9.8 %custom-call.23 = f32[1,128,128]{1,2,0:T(8,128)S(1)} custom-call(f32[1,128,128]{2,1,0:T(8,128)S(1)} %get-tuple-element.92), custom_call_target="InvertDiagBlocksLowerTriangular" | custom-call | tf_op jit(solution)/shard_map/jit(cholesky)/cholesky | solution.py:49
  249.6 11.7 %cholesky.147 = f32[128,128]{1,0:T(8,128)S(1)} custom-call(f32[128,128]{1,0:T(8,128)S(1)} %convolution_subtract_fusion.6), custom_call_target="Cholesky" | custom-call | tf_op jit(solution)/shard_map/jit(cholesky)/cholesky | solution.py:49
  264.2 4.2 while.5
  265.0 1.3 bitcast_dynamic-update-slice_fusion.4
  267.0 1.3 bitcast_dynamic-update-slice_fusion.4
  268.4 19.7 %custom-call.20 = f32[2,128,128]{1,2,0:T(8,128)S(1)} custom-call(f32[2,128,128]{2,1,0:T(8,128)S(1)} %get-tuple-element.49), custom_call_target="InvertDiagBlocksLowerTriangular" | custom-call | tf_op jit(solution)/shard_map/triangular_solve | solution.py:50
  288.1 1.3 broadcast_select_fusion.1
  292.1 20.1 %convolution_bitcast_fusion = f32[6144,256]{0,1:T(8,128)} fusion(f32[6144,768]{1,0:T(8,128)} %param.8, f32[128,768]{1,0:T(8,128)S(1)} %fusion.42, f32[128,768]{1,0:T(8,128)S(1)} %fusion.10, s32[768]{0:T(1024)S(1)} %fusion.50), kind=kOutput, calls=%fused_computation.6 | convolution fusion | flops 14496301056 | bytes 25955328 | tf_op jit(solution)/shard_map/dot_general | solution.py:21
  312.7 1.7 slice_select_fusion.2
  314.3 4.8 fusion.2
  319.2 5.1 convolution_subtract_fusion
  324.3 3.1 fusion.44
  327.4 1.7 copy-done.1
  329.1 22.4 %fusion.9 = f32[256,768]{1,0:T(8,128)} fusion(f32[6144,768]{1,0:T(8,128)} %param.8, f32[6144,128]{0,1:T(8,128)S(1)} %fusion.44, f32[6144,128]{0,1:T(8,128)S(1)} %fusion.2, s32[6144]{0:T(1024)S(1)} %fusion.48), kind=kOutput, calls=%fused_computation.34 | convolution fusion | flops 14501806080 | bytes 25976832 | tf_op jit(solution)/shard_map/dot_general | solution.py:21
  351.5 99.9 %all-reduce.11.cloned.1.call-done = f32[6144,256]{0,1:T(8,128)} async-done(((f32[6144,256]{0,1:T(8,128)}), f32[6144,256]{0,1:T(8,128)}) %all-reduce.11.cloned.1.call-update) | async-done | bytes 6291472 | tf_op jit(solution)/shard_map/psum | solution.py:70
  451.3 15.9 %fusion.8 = f32[256,256]{1,0:T(8,128)} fusion(f32[6144,256]{0,1:T(8,128)} %all-reduce.11.cloned.1.call-done, f32[6144,128]{0,1:T(8,128)} %copy-done.1, f32[6144,128]{0,1:T(8,128)S(1)} %fusion.2, s32[6144]{0:T(1024)} %copy-done.11), kind=kOutput, calls=%fused_computation.33 | convolution fusion | flops 4838129664 | bytes 12869632 | tf_op jit(solution)/shard_map/dot_general | solution.py:21
  468.2 45.4 %all-reduce.13.cloned.1.call-done = (f32[256,768]{1,0:T(8,128)}, f32[256,256]{0,1:T(8,128)}, f32[256,256]{1,0:T(8,128)}) async-done(((f32[256,768]{1,0:T(8,128)}, f32[256,256]{0,1:T(8,128)}, f32[256,256]{1,0:T(8,128)}), (f32[256,768]{1,0:T(8,128)}, f32[256,256]{0,1:T(8,128)}, f32[256,256]{1,0:T(8,128)})) %all-reduce.13.cloned.1.call-update) | async-done | bytes 1310736 | tf_op jit(solution)/shard_map/psum | solution.py:74
  513.6 1.2 fusion.21
  514.8 1.2 convolution_subtract_fusion.4
  516.0 1.2 fusion.43
  517.2 1.1 fusion.18
  519.1 1.8 copy.17
  520.9 1.1 fusion.13
  523.3 13.2 %cholesky.164 = f32[128,128]{1,0:T(8,128)} custom-call(f32[128,128]{1,0:T(8,128)} %cholesky.197), custom_call_target="Cholesky" | custom-call | tf_op jit(solution)/shard_map/jit(cholesky)/cholesky | solution.py:65
  536.4 2.0 select_reduce_fusion.1
  538.4 1.6 cholesky.189
  540.0 11.3 %custom-call.24 = f32[1,128,128]{1,2,0:T(8,128)} custom-call(f32[1,128,128]{2,1,0:T(8,128)} %get-tuple-element.88), custom_call_target="InvertDiagBlocksLowerTriangular" | custom-call | tf_op jit(solution)/shard_map/jit(cholesky)/cholesky | solution.py:65
  551.3 1.7 constant_dynamic-update-slice_fusion.1
  553.0 1.7 convolution_subtract_fusion.5
  554.7 13.2 %cholesky.181 = f32[128,128]{1,0:T(8,128)} custom-call(f32[128,128]{1,0:T(8,128)} %convolution_subtract_fusion.5), custom_call_target="Cholesky" | custom-call | tf_op jit(solution)/shard_map/jit(cholesky)/cholesky | solution.py:65
  567.9 1.5 select_reduce_fusion
  570.0 1.3 compare_reduce_fusion.2
  572.6 1.7 select_select_fusion.1
  575.0 8.6 %while.6 = (s32[]{:T(128)}, f32[256,256]{1,0:T(8,128)}, s32[2,2]{1,0:T(2,128)}, f32[2,128,128]{2,1,0:T(8,128)}, s32[]{:T(128)}) while((s32[]{:T(128)}, f32[256,256]{1,0:T(8,128)}, s32[2,2]{1,0:T(2,128)}, f32[2,128,128]{2,1,0:T(8,128)}, s32[]{:T(128)}) %tuple.70), condition=%wide.while_cond.4, body=%wide.while_body.4.sunk | while | flops 2 | bytes 132705 | solution.py:67
  576.3 3.0 bitcast_dynamic-update-slice_fusion.5
  580.6 2.9 bitcast_dynamic-update-slice_fusion.5
  583.6 21.5 %custom-call.21 = f32[2,128,128]{1,2,0:T(8,128)} custom-call(f32[2,128,128]{2,1,0:T(8,128)} %get-tuple-element.57), custom_call_target="InvertDiagBlocksLowerTriangular" | custom-call | tf_op jit(solution)/shard_map/triangular_solve | solution.py:67
  605.0 1.2 fusion.19
  606.3 1.2 convolution_subtract_fusion.3
  607.5 1.1 fusion.39
  608.7 1.1 fusion.38
  609.8 1.1 convolution_subtract_fusion.2
  610.9 1.1 fusion.37
  612.0 1.3 fusion.29
  613.8 2.0 fusion.30
  615.8 12.9 %fusion.27 = f32[6144,256]{1,0:T(8,128)S(1)} fusion(f32[6144,256]{0,1:T(8,128)} %all-reduce.11.cloned.1.call-done, f32[128,256]{1,0:T(8,128)S(1)} %fusion.38, f32[128,256]{1,0:T(8,128)S(1)} %fusion.37), kind=kOutput, calls=%fused_computation.63 | convolution fusion | flops 4831903744 | bytes 12845056 | tf_op jit(solution)/shard_map/dot_general | solution.py:21
  628.7 12.3 %fusion = f32[6144,256]{1,0:T(8,128)} fusion(f32[6144,256]{1,0:T(8,128)S(1)} %fusion.27, f32[256,256]{1,0:T(8,128)S(1)} %fusion.28, f32[6144,128]{0,1:T(8,128)S(1)} %copy-done.2, f32[6144,128]{0,1:T(8,128)S(1)} %fusion.2, s32[6144]{0:T(1024)S(1)} %copy-done.12), kind=kOutput, calls=%fused_computation.8 | convolution fusion | flops 4841275392 | bytes 19161088 | tf_op jit(solution)/shard_map/dot_general | solution.py:21
  641.0 1.0 fusion.6
  642.0 19.0 %fusion.7 = f32[6144,768]{0,1:T(8,128)} fusion(f32[256,768]{1,0:T(8,128)S(1)} %fusion.6, f32[6144,128]{0,1:T(8,128)S(1)} %copy-done.2, f32[6144,128]{0,1:T(8,128)S(1)} %fusion.2, s32[6144]{0:T(1024)S(1)} %copy-done.12), kind=kOutput, calls=%fused_computation.32 | convolution fusion | flops 14501806080 | bytes 25976832 | tf_op jit(solution)/shard_map/dot_general | solution.py:21
  661.0 28.5 %subtract_subtract_fusion = f32[6144,768]{0,1:T(8,128)} fusion(f32[6144,768]{0,1:T(8,128)} %copy.19, f32[6144,768]{0,1:T(8,128)} %fusion.7, f32[6144,256]{1,0:T(8,128)} %fusion, f32[128,768]{1,0:T(8,128)S(1)} %copy-done.4, f32[128,768]{1,0:T(8,128)S(1)} %fusion.10, s32[768]{0:T(1024)S(1)} %fusion.50), kind=kOutput, calls=%fused_computation.4 | convolution fusion | flops 14505738240 | bytes 63704064 | tf_op jit(solution)/shard_map/dot_general | solution.py:21
  689.5 7.3 %fusion.1 = f32[6144,768]{0,1:T(8,128)} fusion(f32[6144,768]{0,1:T(8,128)} %subtract_subtract_fusion, f32[256,256]{0,1:T(8,128)S(1)} %copy-done.10, pred[]{:T(512)} %compare_reduce_fusion.5, pred[]{:T(512)S(6)} %eq.24, pred[6144]{0:T(1024)(128)(4,1)S(1)} %fusion.49), kind=kLoop, calls=%fused_computation.10 | loop fusion | flops 4718592 | bytes 12851713 | tf_op jit(solution)/shard_map/scatter | solution.py:92
  696.8 2.6 fusion.5
  699.3 18.6 %copy.23 = f32[6144,768]{1,0:T(8,128)} copy(f32[6144,768]{0,1:T(8,128)} %fusion.5) | data formatting | bytes 37748736 | tf_op jit(solution)/shard_map/scatter | solution.py:98
  (69 shorter events, 14.2 us)
Async XLA Ops:
  6.5 166.6 %all-reduce.9.cloned.1.call-start = ((), (), s32[]{:S(2)}) async-start(), calls=%async_computation | async-start | bytes 12582912 | tf_op jit(solution)/shard_map/psum | solution.py:17
  31.3 194.2 %all-reduce.15.cloned.1.call-start = ((), (), s32[]{:S(2)}) async-start(), calls=%async_computation.3 | async-start | bytes 2097152 | tf_op jit(solution)/shard_map/psum | solution.py:48
  176.4 2.7 copy-start
  185.0 266.3 %all-reduce.11.cloned.1.call-start = ((), (), s32[]{:S(2)}) async-start(), calls=%async_computation.1 | async-start | bytes 12582912 | tf_op jit(solution)/shard_map/psum | solution.py:70
  261.4 7.0 copy-start.8
  268.4 43.8 %copy-start.5 = (f32[256,256]{1,0:T(8,128)}, f32[256,256]{1,0:T(8,128)S(1)}, u32[]{:S(2)}) copy-start(f32[256,256]{1,0:T(8,128)S(1)} %get-tuple-element.209) | copy-start | bytes 786436
  268.4 43.7 %copy-start.14 = (s32[2,2]{1,0:T(2,128)}, s32[2,2]{1,0:T(2,128)S(1)}, u32[]{:S(2)}) copy-start(s32[2,2]{1,0:T(2,128)S(1)} %get-tuple-element.221) | copy-start | bytes 52
  288.1 24.1 %copy-start.6 = (f32[2,128,128]{1,2,0:T(8,128)}, f32[2,128,128]{1,2,0:T(8,128)S(1)}, u32[]{:S(2)}) copy-start(f32[2,128,128]{1,2,0:T(8,128)S(1)} %custom-call.20) | copy-start | bytes 393220
  291.3 0.7 copy-start.3
  312.2 201.4 %all-reduce.13.cloned.1.call-start = ((), (), s32[]{:S(2)}) async-start(), calls=%async_computation.2 | async-start | bytes 2621440 | tf_op jit(solution)/shard_map/psum | solution.py:74
  312.7 14.7 %copy-start.11 = (s32[6144]{0:T(1024)}, s32[6144]{0:T(1024)S(1)}, u32[]{:S(2)}) copy-start(s32[6144]{0:T(1024)S(1)} %fusion.48) | copy-start | bytes 73732
  319.2 5.1 copy-start.7
  327.4 1.7 copy-start.1
  521.9 0.7 copy-start.13
  615.8 12.9 %copy-start.2 = (f32[6144,128]{0,1:T(8,128)S(1)}, f32[6144,128]{0,1:T(8,128)}, u32[]{:S(2)}) copy-start(f32[6144,128]{0,1:T(8,128)} %copy-done.1) | copy-start | bytes 9437188
  615.8 12.9 %copy-start.12 = (s32[6144]{0:T(1024)S(1)}, s32[6144]{0:T(1024)}, u32[]{:S(2)}) copy-start(s32[6144]{0:T(1024)} %copy-done.11) | copy-start | bytes 73732
  628.7 12.3 %copy-start.4 = (f32[128,768]{1,0:T(8,128)S(1)}, f32[128,768]{1,0:T(8,128)}, u32[]{:S(2)}) copy-start(f32[128,768]{1,0:T(8,128)} %copy-done.3) | copy-start | bytes 1179652
  661.0 28.5 %copy-start.10 = (f32[256,256]{0,1:T(8,128)S(1)}, f32[256,256]{0,1:T(8,128)}, u32[]{:S(2)}) copy-start(f32[256,256]{0,1:T(8,128)} %get-tuple-element.83) | copy-start | bytes 786436
  689.5 7.3 %copy-start.9 = (f32[256,256]{1,0:T(8,128)S(1)}, f32[256,256]{1,0:T(8,128)}, u32[]{:S(2)}) copy-start(f32[256,256]{1,0:T(8,128)} %copy-done.8) | copy-start | bytes 786436
Sparse Core Ops, SparseCore 0:
  31.4 141.7 all-reduce.8
  185.2 40.2 all-reduce.14
  312.3 138.9 all-reduce.10
  467.4 46.1 all-reduce.12
where the time goes:
time: 732 us; the launch traced here: 725 us
  waiting for transfers between devices  325 us (44%)
  matrix products  175 us (24%)
  other arithmetic  146 us (20%)
  local copies, waits for them, and re-layouts  61.4 us (8%)
  between operations  16.3 us (2%)
    dot_general x14, matrix products, contract(): lax.dot_general(left_op, right_op, (((left_dim,), (right_dim,)), ((), ())...  145 us
    psum x1, waiting for transfers between devices, from_root(): return lax.psum(kept, axis)  140 us
    psum x1, waiting for transfers between devices, per_device(): u_row = lax.psum(contract(current, reflector_t, 1, 1), 'col')  99.9 us
    psum x1, waiting for transfers between devices, per_device(): ut_col = lax.psum(contract(reflector, current, 0, 0), 'row')  45.4 us
    another operation x7, other arithmetic, per_device(): normal_chol = jnp.linalg.cholesky(normal_mat)  43.1 us
    psum x1, waiting for transfers between devices, per_device(): gram, leading_rows = lax.psum((gram_part, leading_part), 'row')  40.2 us
    another operation x6, other arithmetic, per_device(): lower_factor = jnp.linalg.cholesky(gram)  34 us
    unnamed x33, local copies, waits for them, and re-layouts  25.2 us
  transfers between devices with their start and end apart: 4, of which 4 were waited for; matrix products, arithmetic and copies ran while one was open for 6% of the time, Pallas kernels for 0%

commit v1 on v0

v1 whole, which is shorter than its diff:
```python
import math

import jax
import jax.numpy as jnp
from jax import lax
from jax.experimental import pallas as pl
from jax.experimental.pallas import tpu as pltpu
from jax.sharding import PartitionSpec as P

B = 256
NB = 64
TILE = 512
HIGH = lax.Precision.HIGH
HIGHEST = lax.Precision.HIGHEST
VMEM = pl.BlockSpec(memory_space=pltpu.VMEM)


def contract(left_op, right_op, left_dim, right_dim, precision=HIGHEST):
    return lax.dot_general(
        left_op,
        right_op,
        (((left_dim,), (right_dim,)), ((), ())),
        precision=precision,
        preferred_element_type=jnp.float32,
    )


def eye(n):
    rows = lax.broadcasted_iota(jnp.int32, (n, n), 0)
    cols = lax.broadcasted_iota(jnp.int32, (n, n), 1)
    return (rows == cols).astype(jnp.float32)


def eliminate(block, full):
    whole = jnp.concatenate([block, eye(NB)], axis=1)
    parts = [whole[8 * g : 8 * g + 8] for g in range(NB // 8)]
    sub = lax.broadcasted_iota(jnp.int32, (8, 2 * NB), 0)
    for j in range(NB):
        home, at = j // 8, j % 8
        row = parts[home][at : at + 1, :]
        scaled = row * (1.0 / row[:, j : j + 1])
        for g in range(0 if full else home, NB // 8):
            moved = parts[g] - parts[g][:, j : j + 1] * scaled
            if g == home:
                if full:
                    moved = jnp.where(sub == at, scaled, moved)
                else:
                    moved = jnp.where(sub > at, moved, parts[g])
            parts[g] = moved
    return jnp.concatenate(parts, axis=0)


def factor_kernel(gram_ref, r_ref, linv_ref, work):
    work[:, :B] = gram_ref[...]
    work[:, B:] = eye(B)
    for o in range(0, B, NB):
        done = eliminate(work[o : o + NB, o : o + NB], False)
        diag = jnp.sum(done[:, :NB] * eye(NB), axis=1, keepdims=True)
        scaled = done[:, NB:] * lax.rsqrt(diag)
        strip = contract(scaled, work[o : o + NB, :], 1, 0)
        rows = o + lax.broadcasted_iota(jnp.int32, (NB, B), 0)
        cols = lax.broadcasted_iota(jnp.int32, (NB, B), 1)
        r_ref[o : o + NB, :] = jnp.where(cols >= rows, strip[:, :B], 0.0)
        linv_ref[o : o + NB, :] = strip[:, B:]
        if o + NB < B:
            below = contract(strip[:, :B], strip, 0, 0)
            work[o + NB :, :] = work[o + NB :, :] - below[o + NB :, :]


def factor(gram):
    out = jax.ShapeDtypeStruct((B, B), jnp.float32)
    return pl.pallas_call(
        factor_kernel,
        out_shape=(out, out),
        in_specs=[VMEM],
        out_specs=(VMEM, VMEM),
        scratch_shapes=[pltpu.VMEM((B, 2 * B), jnp.float32)],
    )(gram)


def inverse_kernel(lead_t_ref, linv_ref, t_ref, work):
    work[:, :B] = eye(B) - contract(lead_t_ref[...], linv_ref[...], 0, 1)
    work[:, B:] = eye(B)
    for o in range(0, B, NB):
        done = eliminate(work[o : o + NB, o : o + NB], True)
        strip = contract(done[:, NB:], work[o : o + NB, :], 1, 0)
        change = contract(work[:, o : o + NB], strip, 1, 0)
        work[...] = work[...] - change
        work[o : o + NB, :] = strip
    t_ref[...] = work[:, B:]


def inverse(lead_t, linv):
    return pl.pallas_call(
        inverse_kernel,
        out_shape=jax.ShapeDtypeStruct((B, B), jnp.float32),
        in_specs=[VMEM, VMEM],
        out_specs=VMEM,
        scratch_shapes=[pltpu.VMEM((B, 2 * B), jnp.float32)],
    )(lead_t, linv)


def split(value):
    high = value.astype(jnp.bfloat16)
    low = (value - high.astype(jnp.float32)).astype(jnp.bfloat16)
    return high, low


def update_kernel(scale, a_ref, p_ref, u_ref, x1_ref, y_ref, x_ref, r_ref, o_ref, right):
    step = pl.program_id(0)
    row_at = lax.axis_index("row")
    col_at = lax.axis_index("col")
    cols_dev = a_ref.shape[1]

    @pl.when(step == 0)
    def _():
        for at, ref in ((0, x1_ref), (3, y_ref)):
            high, low = split(ref[...])
            right[at * B : (at + 1) * B, :] = high
            right[(at + 1) * B : (at + 2) * B, :] = high
            right[(at + 2) * B : (at + 3) * B, :] = low

    p_high, p_low = split(p_ref[...])
    u_high, u_low = split(u_ref[...])
    left = jnp.concatenate([p_high, p_low, p_high, u_high, u_low, u_high], axis=1)
    o_ref[...] = a_ref[...] - jnp.dot(left, right[...], preferred_element_type=jnp.float32)

    first = jnp.logical_and(step == 0, row_at == 0)

    @pl.when(first)
    def _():
        o_ref[B : 2 * B, :] = o_ref[B : 2 * B, :] + x_ref[...]
        global_cols = col_at * cols_dev + lax.broadcasted_iota(jnp.int32, (B, cols_dev), 1)
        band = lax.broadcasted_iota(jnp.int32, (B, cols_dev), 0)
        onehot = (global_cols - B == band).astype(jnp.float32)
        mirror = contract(r_ref[...] * scale, onehot, 0, 0)
        o_ref[:B, :] = jnp.where(global_cols >= B, mirror, o_ref[:B, :])

    @pl.when(jnp.logical_and(first, col_at == 0))
    def _():
        o_ref[B : 2 * B, :B] = r_ref[...] * scale

    @pl.when(jnp.logical_and(jnp.logical_not(first), col_at == 0))
    def _():
        o_ref[:, :B] = jnp.zeros((TILE, B), jnp.float32)


def update(current, panel, u_rows, x1, y, x, r_mat, order):
    rows_dev, cols_dev = current.shape
    tall = pl.BlockSpec((TILE, B), lambda i: (i, 0))
    flat = pl.BlockSpec((B, cols_dev), lambda i: (0, 0))
    wide = pl.BlockSpec((TILE, cols_dev), lambda i: (i, 0))
    scale = 1.0 / math.sqrt(order)

    def kernel(*refs):
        update_kernel(scale, *refs)

    return pl.pallas_call(
        kernel,
        grid=(rows_dev // TILE,),
        out_shape=jax.ShapeDtypeStruct((rows_dev, cols_dev), jnp.float32),
        in_specs=[wide, tall, tall, flat, flat, flat, pl.BlockSpec((B, B), lambda i: (0, 0))],
        out_specs=wide,
        scratch_shapes=[pltpu.VMEM((6 * B, cols_dev), jnp.bfloat16)],
        compiler_params=pltpu.CompilerParams(vmem_limit_bytes=48 * 1024 * 1024),
    )(current, panel, u_rows, x1, y, x, r_mat)


def spread(chunk, n_row, n_col, same_plane):
    rows = chunk.shape[0] // n_row
    piece = None
    for h in range(n_row):
        pairs = []
        for g in range(h, n_row * n_col, n_row):
            plane = g // n_col if same_plane else 0
            pairs.append((plane * n_col + g // n_row, g))
        moved = lax.ppermute(chunk[h * rows : (h + 1) * rows], ("row", "col"), pairs)
        piece = moved if piece is None else piece + moved
    return lax.all_gather(piece, "col", axis=0, tiled=True)


def per_device(n_row, n_col, symmetric):
    rows_dev, cols_dev = symmetric.shape
    order = cols_dev * n_col
    row_at = lax.axis_index("row")
    col_at = lax.axis_index("col")
    global_cols = col_at * cols_dev + jnp.arange(cols_dev, dtype=jnp.int32)
    band_index = jnp.arange(B, dtype=jnp.int32)
    is_top = row_at == 0

    strip = jnp.where((global_cols >= B)[None, :], symmetric[:B], jnp.float32(0.0))
    col_unit = (band_index[:, None] == global_cols[None, :] - B).astype(jnp.float32)
    panel = spread(strip.T, n_row, n_col, False)

    own = jnp.where(is_top, strip, jnp.float32(0.0))
    gram_part = contract(own, own, 1, 1)
    lead_part = contract(own, col_unit, 1, 1)
    gram, lead_t = lax.psum((gram_part, lead_part), ("row", "col"))
    tops = jnp.concatenate([own, jnp.where(is_top, symmetric[B : 2 * B], 0.0)], axis=0)
    tops = lax.psum(tops, "row")
    p_col, e_col = tops[:B], tops[B:]

    r_mat, linv = factor(gram)
    t_mat = inverse(lead_t, linv)
    v_col = contract(linv, p_col, 1, 0) - col_unit

    q_col = lax.psum(contract(panel, symmetric, 0, 0, HIGH), "row")
    u_col = contract(linv, q_col, 1, 0) - e_col
    u_rows = spread(u_col.T, n_row, n_col, True)
    core_sum = lax.psum(contract(v_col, u_col, 1, 1), "col")
    middle = contract(contract(t_mat, core_sum, 1, 0), t_mat, 1, 1)
    x = contract(t_mat, u_col, 1, 0) - contract(middle, v_col, 1, 0)
    y = contract(t_mat, v_col, 0, 0)
    x1 = contract(linv, x, 0, 0)
    return update(symmetric, panel, u_rows, x1, y, x, r_mat, order)


def solution(mesh):
    n_row, n_col = mesh.shape["row"], mesh.shape["col"]

    def run(symmetric):
        return per_device(n_row, n_col, symmetric)

    return jax.shard_map(
        run, mesh=mesh, in_specs=(P("row", "col"),), out_specs=P("row", "col"), check_vma=False
    )
```

time: 732 us -> 457 us (0.62)
  other arithmetic: 146 us -> 4.22 us
  matrix products: 175 us -> 34.6 us
  Pallas kernels: 0 us -> 79.7 us
  local copies, waits for them, and re-layouts: 61.4 us -> 2.11 us
  waiting for transfers between devices: 325 us -> 314 us
    psum x4 -> x3, waiting for transfers between devices: 325 us -> 177 us  [the longest x1 74.5 us: per_device(): gram, lead_t = lax.psum((gram_part, lead_part), ('row', 'col'))]
    all_gather x0 -> x2, waiting for transfers between devices: none -> 137 us  [spread(): return lax.all_gather(piece, 'col', axis=0, tiled=True)]
    another operation x18 -> x0, other arithmetic: 121 us -> none  [the longest x7 43.1 us: per_device(): normal_chol = jnp.linalg.cholesky(normal_mat)]
    dot_general x14 -> x12, matrix products: 145 us -> 34.6 us  [contract(): lax.dot_general(left_op, right_op, (((left_dim,), (right_dim,)), ((), ())...]
    pallas_call x0 -> x3, Pallas kernels: none -> 79.7 us  [the longest x1 27.3 us: inverse(): pl.pallas_call(inverse_kernel, out_shape=jax.ShapeDtypeStruct((B, B), jnp...]
    another operation x19 -> x0, matrix products: 29.3 us -> none  [the longest x3 13 us: per_device(): lax.linalg.triangular_solve(lower_factor, panel_cols, left_side=False, lo...]
    unnamed x33 -> x6, local copies, waits for them, and re-layouts: 25.2 us -> 0.54 us
    scatter x1 -> x0, local copies, waits for them, and re-layouts: 18.6 us -> none  [per_device(): current = current.at[first_col:first_col + B, :].set(new_top)]
  transfers between devices with their start and end apart: 4 -> 9, of which waited for: 4 -> 6; matrix products, arithmetic and copies ran while one was open for 6% -> 7% of each run, Pallas kernels for 0% -> 12%
where the time goes in v1:
time: 457 us
  waiting for transfers between devices  314 us (69%)
  Pallas kernels  79.7 us (17%)
  matrix products  34.6 us (8%)
  between operations  14.7 us (3%)
  starting transfers between devices  6.84 us (1%)
    all_gather x2, waiting for transfers between devices, spread(): return lax.all_gather(piece, 'col', axis=0, tiled=True)  137 us
    psum x1, waiting for transfers between devices, per_device(): gram, lead_t = lax.psum((gram_part, lead_part), ('row', 'col'))  74.5 us
    psum x1, waiting for transfers between devices, per_device(): core_sum = lax.psum(contract(v_col, u_col, 1, 1), 'col')  58.7 us
    psum x1, waiting for transfers between devices, per_device(): q_col = lax.psum(contract(panel, symmetric, 0, 0, HIGH), 'row')  43.7 us
    dot_general x12, matrix products, contract(): lax.dot_general(left_op, right_op, (((left_dim,), (right_dim,)), ((), ())...  34.6 us
    pallas_call x1, Pallas kernels, inverse(): pl.pallas_call(inverse_kernel, out_shape=jax.ShapeDtypeStruct((B, B), jnp...  27.3 us
    pallas_call x1, Pallas kernels, factor(): pl.pallas_call(factor_kernel, out_shape=(out, out), in_specs=[VMEM], out_...  26.3 us
    pallas_call x1, Pallas kernels, update(): pl.pallas_call(kernel, grid=(rows_dev // TILE,), out_shape=jax.ShapeDtype...  26.1 us
  transfers between devices with their start and end apart: 9, of which 6 were waited for; matrix products, arithmetic and copies ran while one was open for 7% of the time, Pallas kernels for 12%

profile of v1, /device:TPU:0, one launch (start us, length us, event | category | flops | bytes accessed | tf_op | source)
XLA Modules:
  0.0 456.6 jit_solution(13868113959830299986)
XLA Ops:
  7.4 0.0 all-gather.3.cloned.1.call-start
  7.4 1.5 fusion.5
  8.9 0.3 copy.6
  9.1 0.2 select_select_fusion
  9.3 0.1 fusion.7
  9.4 2.4 collective-permute-start.1
  11.8 0.7 collective-permute-start
  12.4 0.6 collective-permute-done.1
  13.1 0.0 collective-permute-done
  13.1 0.8 add.37
  13.9 0.0 all-gather.3.cloned.1.call-update
  13.9 0.0 all-reduce.8.cloned.1.call-start
  14.0 1.5 fusion.1
  15.5 2.1 fusion.8
  17.6 0.0 all-reduce.8.cloned.1.call-update
  17.6 0.0 all-reduce.10.cloned.1.call-start
  17.6 0.3 copy.7
  17.9 0.1 broadcast_select_fusion
  18.0 1.4 pad_maximum_fusion
  19.3 78.0 %all-gather.3.cloned.1.call-done.refs_1_ = f32[6144,256]{1,0:T(8,128)} async-done(((f32[384,256]{1,0:T(8,128)}), f32[6144,256]{1,0:T(8,128)}) %all-gather.3.cloned.1.call-update) | async-done | bytes 6291472 | tf_op jit(solution)/shard_map/all_gather | solution.py:179
  97.3 14.3 %fusion.9 = f32[256,768]{1,0:T(8,128)} fusion(f32[6144,256]{1,0:T(8,128)} %all-gather.3.cloned.1.call-done.refs_1_, f32[6144,768]{1,0:T(8,128)} %refs_0_.1), kind=kOutput, calls=%fused_computation.18 | convolution fusion | flops 7247757312 | bytes 25952256 | tf_op jit(solution)/shard_map/dot_general | solution.py:19
  111.6 0.0 all-reduce.10.cloned.1.call-update
  111.6 0.2 all-reduce.6.cloned.1.call-start
  111.9 74.5 %all-reduce.8.cloned.1.call-done = (f32[256,256]{1,0:T(8,128)}, f32[256,256]{1,0:T(8,128)}) async-done(((f32[256,256]{1,0:T(8,128)}, f32[256,256]{1,0:T(8,128)}), (f32[256,256]{1,0:T(8,128)}, f32[256,256]{1,0:T(8,128)})) %all-reduce.8.cloned.1.call-update) | async-done | bytes 524304 | tf_op jit(solution)/shard_map/psum | solution.py:198
  186.4 26.3 %shard_map.17 = (f32[256,256]{1,0:T(8,128)}, f32[256,256]{1,0:T(8,128)}) custom-call(f32[256,256]{1,0:T(8,128)} %get-tuple-element.9.gram_ref), custom_call_target="tpu_custom_call" | custom-call | tf_op jit(solution)/shard_map/pallas_call | solution.py:72
  212.7 43.7 %all-reduce.10.cloned.1.call-done = (f32[256,768]{1,0:T(8,128)}, f32[512,768]{0,1:T(8,128)}) async-done(((f32[256,768]{1,0:T(8,128)}, f32[512,768]{0,1:T(8,128)}), (f32[256,768]{1,0:T(8,128)}, f32[512,768]{0,1:T(8,128)})) %all-reduce.10.cloned.1.call-update) | async-done | bytes 2359312 | tf_op jit(solution)/shard_map/psum | solution.py:207
  256.4 2.1 convolution_subtract_fusion.1
  258.5 2.9 convolution_subtract_fusion.2
  261.4 0.1 fusion.6
  261.4 0.0 copy-start.1
  261.4 1.8 collective-permute-start.3
  263.2 1.4 collective-permute-start.2
  264.6 1.5 fusion.11
  266.1 0.0 copy-start
  266.1 0.0 all-reduce.6.cloned.1.call-update
  266.2 0.3 all-gather.5.cloned.1.call-start
  266.4 0.0 collective-permute-done.3
  266.5 0.0 collective-permute-done.2
  266.5 1.8 add.38
  268.3 0.0 all-gather.5.cloned.1.call-update
  268.3 27.3 %shard_map.18 = f32[256,256]{1,0:T(8,128)} custom-call(f32[256,256]{1,0:T(8,128)} %get-tuple-element.10.lead_t_ref, f32[256,256]{1,0:T(8,128)} %get-tuple-element.7.linv_ref), custom_call_target="tpu_custom_call" | custom-call | tf_op jit(solution)/shard_map/pallas_call | solution.py:94
  295.6 1.8 fusion.15.refs_4_
  297.4 2.7 fusion.10
  300.0 58.7 %all-reduce.6.cloned.1.call-done = f32[256,256]{1,0:T(8,128)} async-done(((f32[256,256]{1,0:T(8,128)}), f32[256,256]{1,0:T(8,128)}) %all-reduce.6.cloned.1.call-update) | async-done | bytes 262160 | tf_op jit(solution)/shard_map/psum | solution.py:210
  358.7 1.4 fusion.12
  360.1 1.4 fusion.13
  361.5 2.0 convolution_subtract_fusion.refs_5_
  363.5 0.0 copy-done.1
  363.5 1.1 fusion.14.refs_3_
  364.6 58.8 %all-gather.5.cloned.1.call-done.refs_2_ = f32[6144,256]{1,0:T(8,128)} async-done(((f32[384,256]{1,0:T(8,128)}), f32[6144,256]{1,0:T(8,128)}) %all-gather.5.cloned.1.call-update) | async-done | bytes 6291472 | tf_op jit(solution)/shard_map/all_gather | solution.py:179
  423.4 0.0 copy-done
  423.4 26.1 %shard_map.19 = f32[6144,768]{1,0:T(8,128)} custom-call(f32[6144,768]{1,0:T(8,128)} %refs_0_.1, f32[6144,256]{1,0:T(8,128)} %all-gather.3.cloned.1.call-done.refs_1_, f32[6144,256]{1,0:T(8,128)} %all-gather.5.cloned.1.call-done.refs_2_, f32[256,768]{1,0:T(8,128)S(1)} %fusion.14.refs_3_, f32[256,768]{1,0:T(8,128)S(1)} %fusion.15.refs_4_, ...), custom_call_target="tpu_custom_call" | custom-call | tf_op jit(solution)/shard_map/pallas_call | solution.py:158
  (2 shorter events, 0.0 us)
Async XLA Ops:
  7.4 90.0 %all-gather.3.cloned.1.call-start = ((), (), s32[]{:S(2)}) async-start(), calls=%async_computation | async-start | bytes 6684672 | tf_op jit(solution)/shard_map/all_gather | solution.py:179
  9.4 3.7 collective-permute-start.1
  11.8 1.3 collective-permute-start
  13.9 172.5 %all-reduce.8.cloned.1.call-start = ((), (), s32[]{:S(2)}) async-start(), calls=%async_computation.3 | async-start | bytes 1048576 | tf_op jit(solution)/shard_map/psum | solution.py:198
  17.6 238.8 %all-reduce.10.cloned.1.call-start = ((), (), s32[]{:S(2)}) async-start(), calls=%async_computation.4 | async-start | bytes 4718592 | tf_op jit(solution)/shard_map/psum | solution.py:207
  111.6 247.1 %all-reduce.6.cloned.1.call-start = ((), (), s32[]{:S(2)}) async-start(), calls=%async_computation.2 | async-start | bytes 524288 | tf_op jit(solution)/shard_map/psum | solution.py:210
  261.4 102.1 %copy-start.1 = (f32[256,256]{1,0:T(8,128)S(1)}, f32[256,256]{1,0:T(8,128)}, u32[]{:S(2)}) copy-start(f32[256,256]{1,0:T(8,128)} %get-tuple-element.7.linv_ref) | copy-start | bytes 786436
  261.4 5.0 %collective-permute-start.3 = (f32[384,256]{1,0:T(8,128)S(1)}, f32[384,256]{1,0:T(8,128)S(1)}, u32[]{:S(2)}, u32[]{:S(2)}) collective-permute-start(f32[384,256]{1,0:T(8,128)S(1)} %get-tuple-element.17), channel_id=1, source_target_pairs={{0,1},{1,3},{2,5},{3,7},{4,9},{5,11},{6,13},{7,15},{24,17},{25,19}... | collective-permute-start | bytes 1179656 | tf_op jit(solution)/shard_map/ppermute | solution.py:177
  263.2 3.2 collective-permute-start.2
  266.1 157.2 %copy-start = (f32[256,256]{1,0:T(8,128)S(1)}, f32[256,256]{1,0:T(8,128)}, u32[]{:S(2)}) copy-start(f32[256,256]{1,0:T(8,128)} %get-tuple-element.8.refs_6_) | copy-start | bytes 786436
  266.2 157.2 %all-gather.5.cloned.1.call-start = ((), (), s32[]{:S(2)}) async-start(), calls=%async_computation.1 | async-start | bytes 6684672 | tf_op jit(solution)/shard_map/all_gather | solution.py:179
Sparse Core Ops, SparseCore 0:
  14.0 83.2 all-gather.2
  266.3 92.3 all-reduce.5
  361.0 62.3 all-gather.4
Sparse Core Ops, SparseCore 1:
  19.8 166.5 all-reduce.7
  188.7 67.7 all-reduce.9

commit v2 on v1

--- a/solution.py
+++ b/solution.py
@@ -10,6 +10,8 @@
 B = 256
 NB = 64
 TILE = 512
+SUB = 4
+MESH = pl.DeviceIdType.MESH
 HIGH = lax.Precision.HIGH
 HIGHEST = lax.Precision.HIGHEST
 VMEM = pl.BlockSpec(memory_space=pltpu.VMEM)
@@ -50,8 +52,8 @@
     return jnp.concatenate(parts, axis=0)
 
 
-def factor_kernel(gram_ref, r_ref, linv_ref, work):
-    work[:, :B] = gram_ref[...]
+def factor_into(gram, r_ref, linv_ref, work):
+    work[:, :B] = gram
     work[:, B:] = eye(B)
     for o in range(0, B, NB):
         done = eliminate(work[o : o + NB, o : o + NB], False)
@@ -67,19 +69,8 @@
             work[o + NB :, :] = work[o + NB :, :] - below[o + NB :, :]
 
 
-def factor(gram):
-    out = jax.ShapeDtypeStruct((B, B), jnp.float32)
-    return pl.pallas_call(
-        factor_kernel,
-        out_shape=(out, out),
-        in_specs=[VMEM],
-        out_specs=(VMEM, VMEM),
-        scratch_shapes=[pltpu.VMEM((B, 2 * B), jnp.float32)],
-    )(gram)
-
-
-def inverse_kernel(lead_t_ref, linv_ref, t_ref, work):
-    work[:, :B] = eye(B) - contract(lead_t_ref[...], linv_ref[...], 0, 1)
+def inverse_kernel(lead_ref, linv_ref, t_ref, work):
+    work[:, :B] = eye(B) - contract(lead_ref[...], linv_ref[...], 1, 1)
     work[:, B:] = eye(B)
     for o in range(0, B, NB):
         done = eliminate(work[o : o + NB, o : o + NB], True)
@@ -90,14 +81,14 @@
     t_ref[...] = work[:, B:]
 
 
-def inverse(lead_t, linv):
+def inverse(lead, linv):
     return pl.pallas_call(
         inverse_kernel,
         out_shape=jax.ShapeDtypeStruct((B, B), jnp.float32),
         in_specs=[VMEM, VMEM],
         out_specs=VMEM,
         scratch_shapes=[pltpu.VMEM((B, 2 * B), jnp.float32)],
-    )(lead_t, linv)
+    )(lead, linv)
 
 
 def split(value):
@@ -166,60 +157,410 @@
     )(current, panel, u_rows, x1, y, x, r_mat)
 
 
-def spread(chunk, n_row, n_col, same_plane):
-    rows = chunk.shape[0] // n_row
-    piece = None
-    for h in range(n_row):
-        pairs = []
-        for g in range(h, n_row * n_col, n_row):
-            plane = g // n_col if same_plane else 0
-            pairs.append((plane * n_col + g // n_row, g))
-        moved = lax.ppermute(chunk[h * rows : (h + 1) * rows], ("row", "col"), pairs)
-        piece = moved if piece is None else piece + moved
-    return lax.all_gather(piece, "col", axis=0, tiled=True)
-
-
-def per_device(n_row, n_col, symmetric):
-    rows_dev, cols_dev = symmetric.shape
-    order = cols_dev * n_col
-    row_at = lax.axis_index("row")
-    col_at = lax.axis_index("col")
+def ring_of(mesh):
+    coords = [tuple(d.coords) for d in mesh.devices[0][::2]]
+    moving = [i for i in range(3) if len({c[i] for c in coords}) > 1]
+    index = {c: i for i, c in enumerate(coords)}
+    long_axis, short_axis = moving[0], moving[-1]
+    tall = sorted({c[long_axis] for c in coords})
+    flat = sorted({c[short_axis] for c in coords})
+
+    def chip(a, b):
+        at = list(coords[0])
+        at[long_axis], at[short_axis] = tall[a], flat[b]
+        return index[tuple(at)]
+
+    order = [chip(a, 0) for a in range(len(tall) - 1, -1, -1)]
+    for a in range(len(tall)):
+        across = range(1, len(flat)) if a % 2 == 0 else range(len(flat) - 1, 0, -1)
+        order += [chip(a, b) for b in across]
+    return order
+
+
+def look_up(table, at):
+    found = jnp.int32(table[0])
+    for i in range(1, len(table)):
+        found = jnp.where(at == i, jnp.int32(table[i]), found)
+    return found
+
+
+def gather_kernel(ring, n_row, hop, *refs):
+    if hop:
+        first_ref, extra_ref, out_ref, chunk_ref, beside_ref = refs[:5]
+        own_sem, ring_send, ring_recv, sib_send, sib_recv, hop_send, hop_recv, beside_send, beside_recv = refs[5:]
+    else:
+        chunk_ref, out_ref, own_sem, ring_send, ring_recv, sib_send, sib_recv = refs
+    row_at, col_at = lax.axis_index("row"), lax.axis_index("col")
+    n = len(ring)
+    rows = chunk_ref.shape[0]
+    cut = rows // SUB
+    chip, core = col_at // 2, lax.rem(col_at, 2)
+    per_plane = n // n_row
+    place = look_up([ring.index(i) for i in range(n)], chip)
+    way = 1 - 2 * core
+    next_col = 2 * look_up(ring, lax.rem(place + way + n, n)) + core
+    prev_col = 2 * look_up(ring, lax.rem(place - way + n, n)) + core
+    sib_col = 2 * chip + 1 - core
+
+    barrier = pltpu.get_barrier_semaphore()
+    for col in (next_col, prev_col, sib_col):
+        pl.semaphore_signal(barrier, inc=1, device_id=(row_at, col), device_id_type=MESH)
+    if hop:
+        @pl.when(row_at == 0)
+        def _():
+            for other in range(1, n_row):
+                pl.semaphore_signal(barrier, inc=1, device_id=(other, col_at), device_id_type=MESH)
+
+        @pl.when(row_at > 0)
+        def _():
+            pl.semaphore_signal(barrier, inc=1, device_id=(0, col_at), device_id_type=MESH)
+    greetings = 3 + (jnp.where(row_at == 0, n_row - 1, 1) if hop else 0)
+    pl.semaphore_wait(barrier, greetings)
+
+    def window(source, of_core, sub):
+        start = (source * 2 + of_core) * rows + sub * cut
+        return out_ref.at[pl.ds(pl.multiple_of(start, 8), cut)]
+
+    def piece(sub):
+        return chunk_ref.at[pl.ds(sub * cut, cut)]
+
+    def hop_copy(other, sub):
+        return pltpu.make_async_remote_copy(
+            src_ref=first_ref.at[pl.ds(sub * cut, cut)],
+            dst_ref=piece(sub),
+            send_sem=hop_send.at[other - 1, sub],
+            recv_sem=hop_recv.at[sub],
+            device_id=(other, col_at),
+            device_id_type=MESH,
+        )
+
+    def beside_copy(other):
+        return pltpu.make_async_remote_copy(
+            src_ref=extra_ref,
+            dst_ref=beside_ref,
+            send_sem=beside_send.at[other - 1],
+            recv_sem=beside_recv,
+            device_id=(other, col_at),
+            device_id_type=MESH,
+        )
+
+    def ring_copy(source, sub, src):
+        return pltpu.make_async_remote_copy(
+            src_ref=src,
+            dst_ref=window(source, core, sub),
+            send_sem=ring_send.at[source, sub],
+            recv_sem=ring_recv.at[source, sub],
+            device_id=(row_at, next_col),
+            device_id_type=MESH,
+        )
+
+    def sib_copy(source, of_core, sub, src):
+        return pltpu.make_async_remote_copy(
+            src_ref=src,
+            dst_ref=window(source, of_core, sub),
+            send_sem=sib_send.at[source, sub],
+            recv_sem=sib_recv.at[source, sub],
+            device_id=(row_at, sib_col),
+            device_id_type=MESH,
+        )
+
+    def found(step):
+        at = look_up(ring, lax.rem(place - way * step + n, n))
+        source = at - row_at * per_plane
+        valid = jnp.logical_and(source >= 0, source < per_plane)
+        return valid, jnp.clip(source, 0, per_plane - 1)
+
+    if hop:
+        @pl.when(row_at == 0)
+        def _():
+            for sub in range(SUB):
+                for other in range(1, n_row):
+                    hop_copy(other, sub).start()
+            for other in range(1, n_row):
+                beside_copy(other).start()
+            moves = [
+                pltpu.make_async_copy(first_ref, chunk_ref, own_sem.at[0]),
+                pltpu.make_async_copy(extra_ref, beside_ref, own_sem.at[1]),
+            ]
+            for move in moves:
+                move.start()
+            for move in moves:
+                move.wait()
+
+    valid_home, home = found(0)
+
+    def own_copy(sub):
+        return pltpu.make_async_copy(piece(sub), window(home, core, sub), own_sem.at[2 + sub])
+
+    for sub in range(SUB):
+        if hop:
+            @pl.when(row_at > 0)
+            def _():
+                hop_copy(1, sub).wait_recv()
+
+        @pl.when(valid_home)
+        def _():
+            ring_copy(home, sub, piece(sub)).start()
+            sib_copy(home, core, sub, piece(sub)).start()
+            own_copy(sub).start()
+
+    def forward(step, carry):
+        valid, source = found(step)
+
+        @pl.when(valid)
+        def _():
+            for sub in range(SUB):
+                src = window(source, core, sub)
+                ring_copy(source, sub, src).wait_recv()
+
+                @pl.when(step < n - 1)
+                def _():
+                    ring_copy(source, sub, src).start()
+
+                sib_copy(source, core, sub, src).start()
+
+        return carry
+
+    lax.fori_loop(1, n, forward, 0)
+
+    def finish(step, carry):
+        valid, source = found(step)
+
+        @pl.when(valid)
+        def _():
+            for sub in range(SUB):
+                src = window(source, core, sub)
+                sib_copy(source, 1 - core, sub, src).wait_recv()
+
+                @pl.when(step < n - 1)
+                def _():
+                    ring_copy(source, sub, src).wait_send()
+
+                sib_copy(source, core, sub, src).wait_send()
+
+        return carry
+
+    lax.fori_loop(0, n, finish, 0)
+
+    @pl.when(valid_home)
+    def _():
+        for sub in range(SUB):
+            own_copy(sub).wait()
+
+    if hop:
+        @pl.when(row_at == 0)
+        def _():
+            for other in range(1, n_row):
+                for sub in range(SUB):
+                    hop_copy(other, sub).wait_send()
+                beside_copy(other).wait_send()
+
+        @pl.when(row_at > 0)
+        def _():
+            beside_copy(1).wait_recv()
+
+
+def gather(chunks, ring, n_row, hop):
+    per_plane = len(ring) // n_row
+    dma = pltpu.SemaphoreType.DMA
+    rows = chunks[0].shape[0]
+
+    def kernel(*refs):
+        gather_kernel(ring, n_row, hop, *refs)
+
+    whole = jax.ShapeDtypeStruct((rows * per_plane * 2, B), jnp.float32)
+    part = jax.ShapeDtypeStruct((rows, B), jnp.float32)
+    hops = [dma((n_row - 1, SUB)), dma((SUB,)), dma((n_row - 1,)), dma]
+    anywhere = pl.BlockSpec(memory_space=pl.ANY)
+    return pl.pallas_call(
+        kernel,
+        out_shape=(whole, part, part) if hop else whole,
+        in_specs=[anywhere] * len(chunks),
+        out_specs=(anywhere,) * 3 if hop else anywhere,
+        scratch_shapes=[dma((2 + SUB,))] + [dma((per_plane, SUB))] * 4 + (hops if hop else []),
+        compiler_params=pltpu.CompilerParams(collective_id=int(hop), has_side_effects=True),
+    )(*chunks)
+
+
+def peers(n_row, row_at):
+    return [lax.rem(row_at + d, n_row) for d in range(1, n_row)]
+
+
+def greet(n_row, row_at, col_at):
+    barrier = pltpu.get_barrier_semaphore()
+    for other in peers(n_row, row_at):
+        pl.semaphore_signal(barrier, inc=1, device_id=(other, col_at), device_id_type=MESH)
+    pl.semaphore_wait(barrier, n_row - 1)
+
+
+def exchange(n_row, row_at, col_at, src, landing, send, recv):
+    copies = []
+    for at, other in enumerate(peers(n_row, row_at)):
+        copy = pltpu.make_async_remote_copy(
+            src_ref=src,
+            dst_ref=landing.at[at],
+            send_sem=send.at[at],
+            recv_sem=recv.at[at],
+            device_id=(other, col_at),
+            device_id_type=MESH,
+        )
+        copy.start()
+        copies.append(copy)
+    return copies
+
+
+def total(n_row, src, landing, copies):
+    for copy in copies:
+        copy.wait_recv()
+    found = src[...]
+    for at in range(n_row - 1):
+        found = found + landing[at]
+    return found
+
+
+def basis_kernel(
+    n_row, gram_ref, k_ref, lead_ref, p_ref, e_ref, r_ref, linv_ref, lead_out, u_ref, v_ref,
+    work, gram_in, k_in, gram_send, gram_recv, k_send, k_recv, lead_send, lead_recv,
+):
+    row_at, col_at = lax.axis_index("row"), lax.axis_index("col")
+    greet(n_row, row_at, col_at)
+    gram_copies = exchange(n_row, row_at, col_at, gram_ref, gram_in, gram_send, gram_recv)
+
+    def lead_copy(other):
+        return pltpu.make_async_remote_copy(
+            src_ref=lead_ref,
+            dst_ref=lead_out,
+            send_sem=lead_send.at[other - 1],
+            recv_sem=lead_recv,
+            device_id=(other, col_at),
+            device_id_type=MESH,
+        )
+
+    k_copies = exchange(n_row, row_at, col_at, k_ref, k_in, k_send, k_recv)
+
+    @pl.when(row_at == 0)
+    def _():
+        for other in range(1, n_row):
+            lead_copy(other).start()
+        lead_out[...] = lead_ref[...]
+
+    gram = total(n_row, gram_ref, gram_in, gram_copies)
+    factor_into(gram, r_ref, linv_ref, work)
+    linv = linv_ref[...]
+    cols_dev = p_ref.shape[0]
+    global_cols = col_at * cols_dev + lax.broadcasted_iota(jnp.int32, (cols_dev, B), 0)
+    band = lax.broadcasted_iota(jnp.int32, (cols_dev, B), 1)
+    col_unit = (global_cols - B == band).astype(jnp.float32)
+    v_ref[...] = contract(p_ref[...], linv, 1, 1) - col_unit
+    q_col = total(n_row, k_ref, k_in, k_copies)
+    u_ref[...] = contract(q_col, linv, 0, 1) - e_ref[...]
+    for copy in gram_copies + k_copies:
+        copy.wait_send()
+
+    @pl.when(row_at == 0)
+    def _():
+        for other in range(1, n_row):
+            lead_copy(other).wait_send()
+
+    @pl.when(row_at > 0)
+    def _():
+        lead_copy(1).wait_recv()
+
+
+def basis(n_row, gram, k, lead, p_col, e_col):
+    dma = pltpu.SemaphoreType.DMA
+    small = jax.ShapeDtypeStruct((B, B), jnp.float32)
+    part = jax.ShapeDtypeStruct(p_col.shape, jnp.float32)
+    others = dma((n_row - 1,))
+
+    def kernel(*refs):
+        basis_kernel(n_row, *refs)
+
+    return pl.pallas_call(
+        kernel,
+        out_shape=(small, small, small, part, part),
+        in_specs=[VMEM] * 5,
+        out_specs=(VMEM,) * 5,
+        scratch_shapes=[
+            pltpu.VMEM((B, 2 * B), jnp.float32),
+            pltpu.VMEM((n_row - 1, B, B), jnp.float32),
+            pltpu.VMEM((n_row - 1,) + k.shape, jnp.float32),
+            others, others, others, others, others, dma,
+        ],
+        compiler_params=pltpu.CompilerParams(
+            collective_id=2, has_side_effects=True, vmem_limit_bytes=48 * 1024 * 1024
+        ),
+    )(gram, k, lead, p_col, e_col)
+
+
+def middle_kernel(
+    n_row, z_ref, t_ref, linv_ref, u_ref, v_ref, x_ref, x1_ref, y_ref, z_in, z_send, z_recv
+):
+    row_at, col_at = lax.axis_index("row"), lax.axis_index("col")
+    greet(n_row, row_at, col_at)
+    copies = exchange(n_row, row_at, col_at, z_ref, z_in, z_send, z_recv)
+    t_mat = t_ref[...]
+    y_ref[...] = contract(t_mat, v_ref[...], 0, 1)
+    x_ref[...] = contract(t_mat, u_ref[...], 1, 1)
+    core_sum = total(n_row, z_ref, z_in, copies)
+    middle = contract(contract(t_mat, core_sum, 1, 0), t_mat, 1, 1)
+    x = x_ref[...] - contract(middle, v_ref[...], 1, 1)
+    x_ref[...] = x
+    x1_ref[...] = contract(linv_ref[...], x, 0, 0)
+    for copy in copies:
+        copy.wait_send()
+
+
+def middle_terms(n_row, z, t_mat, linv, u_col, v_col):
+    dma = pltpu.SemaphoreType.DMA
+    flat = jax.ShapeDtypeStruct(u_col.shape[::-1], jnp.float32)
+
+    def kernel(*refs):
+        middle_kernel(n_row, *refs)
+
+    return pl.pallas_call(
+        kernel,
+        out_shape=(flat,) * 3,
+        in_specs=[VMEM] * 5,
+        out_specs=(VMEM,) * 3,
+        scratch_shapes=[
+            pltpu.VMEM((n_row - 1, B, B), jnp.float32), dma((n_row - 1,)), dma((n_row - 1,))
+        ],
+        compiler_params=pltpu.CompilerParams(
+            collective_id=3, has_side_effects=True, vmem_limit_bytes=48 * 1024 * 1024
+        ),
+    )(z, t_mat, linv, u_col, v_col)
+
+
+def per_device(ring, n_row, symmetric):
+    cols_dev = symmetric.shape[1]
+    order = symmetric.shape[0] * n_row
+    row_at, col_at = lax.axis_index("row"), lax.axis_index("col")
     global_cols = col_at * cols_dev + jnp.arange(cols_dev, dtype=jnp.int32)
-    band_index = jnp.arange(B, dtype=jnp.int32)
     is_top = row_at == 0
 
     strip = jnp.where((global_cols >= B)[None, :], symmetric[:B], jnp.float32(0.0))
-    col_unit = (band_index[:, None] == global_cols[None, :] - B).astype(jnp.float32)
-    panel = spread(strip.T, n_row, n_col, False)
-
-    own = jnp.where(is_top, strip, jnp.float32(0.0))
-    gram_part = contract(own, own, 1, 1)
-    lead_part = contract(own, col_unit, 1, 1)
-    gram, lead_t = lax.psum((gram_part, lead_part), ("row", "col"))
-    tops = jnp.concatenate([own, jnp.where(is_top, symmetric[B : 2 * B], 0.0)], axis=0)
-    tops = lax.psum(tops, "row")
-    p_col, e_col = tops[:B], tops[B:]
-
-    r_mat, linv = factor(gram)
-    t_mat = inverse(lead_t, linv)
-    v_col = contract(linv, p_col, 1, 0) - col_unit
-
-    q_col = lax.psum(contract(panel, symmetric, 0, 0, HIGH), "row")
-    u_col = contract(linv, q_col, 1, 0) - e_col
-    u_rows = spread(u_col.T, n_row, n_col, True)
-    core_sum = lax.psum(contract(v_col, u_col, 1, 1), "col")
-    middle = contract(contract(t_mat, core_sum, 1, 0), t_mat, 1, 1)
-    x = contract(t_mat, u_col, 1, 0) - contract(middle, v_col, 1, 0)
-    y = contract(t_mat, v_col, 0, 0)
-    x1 = contract(linv, x, 0, 0)
+    panel, p_col, e_col = gather((strip.T, symmetric[B : 2 * B].T), ring, n_row, True)
+    gram_part = contract(panel, panel, 0, 0)
+    k_part = contract(panel, symmetric, 0, 0, HIGH)
+    r_mat, linv, lead, u_col, v_col = basis(
+        n_row, gram_part, k_part, panel[B : 2 * B], p_col, e_col
+    )
+    t_mat = inverse(lead, linv)
+    u_rows = gather((u_col,), ring, n_row, False)
+    z = contract(linv, contract(panel, u_rows, 0, 0), 1, 0)
+    z = z - jnp.where(is_top, u_rows[B : 2 * B], jnp.float32(0.0))
+    x, x1, y = middle_terms(n_row, z, t_mat, linv, u_col, v_col)
     return update(symmetric, panel, u_rows, x1, y, x, r_mat, order)
 
 
 def solution(mesh):
-    n_row, n_col = mesh.shape["row"], mesh.shape["col"]
+    n_row = mesh.shape["row"]
+
+    ring = ring_of(mesh)
 
     def run(symmetric):
-        return per_device(n_row, n_col, symmetric)
+        return per_device(ring, n_row, symmetric)
 
     return jax.shard_map(
         run, mesh=mesh, in_specs=(P("row", "col"),), out_specs=P("row", "col"), check_vma=False

time: 457 us -> 328 us (0.72); the launches traced: 457 us -> 322 us
  waiting for transfers between devices: 314 us -> 0 us
  Pallas kernels: 79.7 us -> 266 us
  between operations: 14.7 us -> 0.4 us
  matrix products: 34.6 us -> 48.7 us
  starting transfers between devices: 6.84 us -> 0 us
    psum x3 -> x0, waiting for transfers between devices: 177 us -> none  [the longest x1 74.5 us: per_device(): gram, lead_t = lax.psum((gram_part, lead_part), ('row', 'col'))]
    pallas_call x1 -> x4, Pallas kernels: 26.3 us -> 201 us  [the longest x2 149 us: gather(): pl.pallas_call(kernel, out_shape=(whole, part, part) if hop else whole, i...]
    all_gather x2 -> x0, waiting for transfers between devices: 137 us -> none  [spread(): return lax.all_gather(piece, 'col', axis=0, tiled=True)]
    dot_general x12 -> x4, matrix products: 34.6 us -> 48.7 us  [contract(): lax.dot_general(left_op, right_op, (((left_dim,), (right_dim,)), ((), ())...]
    pallas_call x1, Pallas kernels: 27.3 us -> 39 us  [inverse(): pl.pallas_call(inverse_kernel, out_shape=jax.ShapeDtypeStruct((B, B), jnp...]
    ppermute x4 -> x0, starting transfers between devices: 6.27 us -> none  [spread(): moved = lax.ppermute(chunk[h * rows:(h + 1) * rows], ('row', 'col'), pairs)]
  transfers between devices with their start and end apart: 9 -> 0, of which waited for: 6 -> 0; matrix products, arithmetic and copies ran while one was open for 7% -> 0% of each run, Pallas kernels for 12% -> 0%
where the time goes in v2:
time: 328 us; the launch traced here: 322 us
  Pallas kernels  266 us (81%)
  matrix products  48.7 us (15%)
  local copies, waits for them, and re-layouts  6.34 us (2%)
    pallas_call x2, Pallas kernels, gather(): pl.pallas_call(kernel, out_shape=(whole, part, part) if hop else whole, i...  149 us
    dot_general x4, matrix products, contract(): lax.dot_general(left_op, right_op, (((left_dim,), (right_dim,)), ((), ())...  48.7 us
    pallas_call x1, Pallas kernels, inverse(): pl.pallas_call(inverse_kernel, out_shape=jax.ShapeDtypeStruct((B, B), jnp...  39 us
    pallas_call x1, Pallas kernels, basis(): pl.pallas_call(kernel, out_shape=(small, small, small, part, part), in_sp...  36.5 us
    pallas_call x1, Pallas kernels, update(): pl.pallas_call(kernel, grid=(rows_dev // TILE,), out_shape=jax.ShapeDtype...  26.1 us
    pallas_call x1, Pallas kernels, middle_terms(): pl.pallas_call(kernel, out_shape=(flat,) * 3, in_specs=[VMEM] * 5, out_sp...  15.4 us

profile of v2, /device:TPU:0, one launch (start us, length us, event | category | flops | bytes accessed | tf_op | source)
XLA Modules:
  0.0 322.3 jit_solution(1597355872202588835)
XLA Ops:
  0.0 1.5 fusion
  1.5 1.2 copy.5
  2.7 0.3 copy.4
  2.9 1.1 select_bitcast_fusion.refs_0_
  4.0 95.6 %shard_map.17 = (f32[6144,256]{1,0:T(8,128)}, f32[768,256]{1,0:T(8,128)}, f32[768,256]{1,0:T(8,128)}) custom-call(f32[768,256]{1,0:T(8,128)} %select_bitcast_fusion.refs_0_, f32[768,256]{1,0:T(8,128)} %bitcast.13), custom_call_target="tpu_custom_call" | custom-call | tf_op jit(solution)/shard_map/pallas_call | solution.py:375
  99.6 0.0 slice-start
  99.6 1.1 slice.14.refs_2_
  100.7 0.0 slice-start.1
  100.7 14.9 %fusion.1.refs_0_ = f32[256,256]{1,0:T(8,128)S(1)} fusion(f32[6144,256]{1,0:T(8,128)} %get-tuple-element.16.refs_1_), kind=kOutput, calls=%fused_computation.4 | convolution fusion | flops 4831838208 | bytes 6553600 | tf_op jit(solution)/shard_map/dot_general | solution.py:21
  115.6 0.0 slice-done
  115.6 0.0 slice-done.1
  115.6 0.0 copy-start.5
  115.7 0.0 copy-start.6
  115.7 18.3 %fusion.2.refs_1_ = f32[256,768]{1,0:T(8,128)S(1)} fusion(f32[6144,256]{1,0:T(8,128)S(1)} %bitcast.12, f32[6144,768]{1,0:T(8,128)} %refs_0_.1), kind=kOutput, calls=%fused_computation.5 | convolution fusion | flops 7247757312 | bytes 25952256 | tf_op jit(solution)/shard_map/dot_general | solution.py:21
  134.0 0.0 copy-done.5
  134.0 0.0 copy-done.6
  134.0 36.5 %shard_map.18 = (f32[256,256]{1,0:T(8,128)S(1)}, f32[256,256]{1,0:T(8,128)S(1)}, f32[256,256]{1,0:T(8,128)S(1)}, f32[768,256]{1,0:T(8,128)S(1)}, f32[768,256]{1,0:T(8,128)S(1)}) custom-call(f32[256,256]{1,0:T(8,128)S(1)} %fusion.1.refs_0_, f32[256,768]{1,0:T(8,128)S(1)} %fusion.2.refs_1_, f32[256,256]{1,0:T(8,128)S(1)} %slice.14.refs_2_, ...), custom_call_target="tpu_custom_call" | custom-call | tf_op jit(solution)/shard_map/pallas_call | solution.py:479
  170.5 0.0 copy-start
  170.5 0.9 copy-done
  171.4 0.0 copy-start.2
  171.4 0.7 copy-done.2
  172.1 0.0 copy-start.7
  172.1 0.7 copy-done.7
  172.8 39.0 %shard_map.20.refs_1_ = f32[256,256]{1,0:T(8,128)} custom-call(f32[256,256]{1,0:T(8,128)} %copy-done.7, f32[256,256]{1,0:T(8,128)} %copy-done.2), custom_call_target="tpu_custom_call" | custom-call | tf_op jit(solution)/shard_map/pallas_call | solution.py:85
  211.8 53.2 %shard_map.19.refs_2_ = f32[6144,256]{1,0:T(8,128)} custom-call(f32[768,256]{1,0:T(8,128)} %copy-done), custom_call_target="tpu_custom_call" | custom-call | tf_op jit(solution)/shard_map/pallas_call | solution.py:375
  265.0 0.0 copy-start.3
  265.0 0.0 copy-start.1
  265.0 0.0 copy-start.4
  265.0 14.2 %fusion.3 = f32[256,256]{1,0:T(8,128)S(1)} fusion(f32[6144,256]{1,0:T(8,128)} %get-tuple-element.16.refs_1_, f32[6144,256]{1,0:T(8,128)} %shard_map.19.refs_2_), kind=kOutput, calls=%fused_computation.6 | convolution fusion | flops 4831838208 | bytes 12845056 | tf_op jit(solution)/shard_map/dot_general | solution.py:21
  279.3 0.0 copy-done.3
  279.3 1.3 convolution_subtract_fusion.refs_0_
  280.6 0.0 copy-done.1
  280.6 0.0 copy-done.4
  280.6 15.4 %shard_map.21 = (f32[256,768]{1,0:T(8,128)S(1)}, f32[256,768]{1,0:T(8,128)S(1)}, f32[256,768]{1,0:T(8,128)S(1)}) custom-call(f32[256,256]{1,0:T(8,128)S(1)} %convolution_subtract_fusion.refs_0_, f32[256,256]{1,0:T(8,128)S(1)} %copy-done.4, f32[256,256]{1,0:T(8,128)S(1)} %copy-done.3, f32[768,256]{1,0:T(8,128)S(1)} %copy-done.1, ...), custom_call_target="tpu_custom_call" | custom-call | tf_op jit(solution)/shard_map/pallas_call | solution.py:521
  296.0 26.1 %shard_map.22 = f32[6144,768]{1,0:T(8,128)} custom-call(f32[6144,768]{1,0:T(8,128)} %refs_0_.1, f32[6144,256]{1,0:T(8,128)} %get-tuple-element.16.refs_1_, f32[6144,256]{1,0:T(8,128)} %shard_map.19.refs_2_, f32[256,768]{1,0:T(8,128)S(1)} %get-tuple-element.23.refs_3_, f32[256,768]{1,0:T(8,128)S(1)} %get-tuple-element.24.refs_4_, ...), custom_call_target="tpu_custom_call" | custom-call | tf_op jit(solution)/shard_map/pallas_call | solution.py:149
  (2 shorter events, 0.0 us)
Async XLA Ops:
  99.6 16.0 %slice-start = ((s8[6291456]{0:T(1024)(128)(4,1)}), s8[4194304]{0:T(1024)(128)(4,1)S(1)}, s32[]{:S(2)}) async-start(s8[6291456]{0:T(1024)(128)(4,1)} %bitcast.11), calls=%async_computation | async-start | bytes 8388608
  100.7 14.9 %slice-start.1 = ((s8[6291456]{0:T(1024)(128)(4,1)}), s8[2097152]{0:T(1024)(128)(4,1)S(1)}, s32[]{:S(2)}) async-start(s8[6291456]{0:T(1024)(128)(4,1)} %bitcast.11), calls=%async_computation.1 | async-start | bytes 4194304
  115.6 18.3 %copy-start.5 = (f32[768,256]{1,0:T(8,128)S(1)}, f32[768,256]{1,0:T(8,128)}, u32[]{:S(2)}) copy-start(f32[768,256]{1,0:T(8,128)} %get-tuple-element.17.refs_3_) | copy-start | bytes 2359300
  115.7 18.3 %copy-start.6 = (f32[768,256]{1,0:T(8,128)S(1)}, f32[768,256]{1,0:T(8,128)}, u32[]{:S(2)}) copy-start(f32[768,256]{1,0:T(8,128)} %get-tuple-element.18.refs_4_) | copy-start | bytes 2359300
  170.5 0.9 copy-start
  171.4 0.7 copy-start.2
  172.1 0.7 copy-start.7
  265.0 14.3 %copy-start.3 = (f32[256,256]{1,0:T(8,128)S(1)}, f32[256,256]{1,0:T(8,128)}, u32[]{:S(2)}) copy-start(f32[256,256]{1,0:T(8,128)} %copy-done.2) | copy-start | bytes 786436
  265.0 15.6 %copy-start.1 = (f32[768,256]{1,0:T(8,128)S(1)}, f32[768,256]{1,0:T(8,128)}, u32[]{:S(2)}) copy-start(f32[768,256]{1,0:T(8,128)} %copy-done) | copy-start | bytes 2359300
  265.0 15.6 %copy-start.4 = (f32[256,256]{1,0:T(8,128)S(1)}, f32[256,256]{1,0:T(8,128)}, u32[]{:S(2)}) copy-start(f32[256,256]{1,0:T(8,128)} %shard_map.20.refs_1_) | copy-start | bytes 786436

commit v3 on v2

v3 whole, which is shorter than its diff:
```python
import math

import jax
import jax.numpy as jnp
from jax import lax
from jax.experimental import pallas as pl
from jax.experimental.pallas import tpu as pltpu
from jax.sharding import PartitionSpec as P

B = 256
NB = 64
TILE = 512
SUB = 8
MESH = pl.DeviceIdType.MESH
HIGH = lax.Precision.HIGH
HIGHEST = lax.Precision.HIGHEST
VMEM = pl.BlockSpec(memory_space=pltpu.VMEM)


def contract(left_op, right_op, left_dim, right_dim, precision=HIGHEST):
    return lax.dot_general(
        left_op,
        right_op,
        (((left_dim,), (right_dim,)), ((), ())),
        precision=precision,
        preferred_element_type=jnp.float32,
    )


def eye(n):
    rows = lax.broadcasted_iota(jnp.int32, (n, n), 0)
    cols = lax.broadcasted_iota(jnp.int32, (n, n), 1)
    return (rows == cols).astype(jnp.float32)


def eliminate_some(whole, columns, full):
    parts = [whole[8 * g : 8 * g + 8] for g in range(NB // 8)]
    sub = lax.broadcasted_iota(jnp.int32, (8, 2 * NB), 0)
    for j in columns:
        home, at = j // 8, j % 8
        row = parts[home][at : at + 1, :]
        scaled = row * (1.0 / row[:, j : j + 1])
        for g in range(0 if full else home, NB // 8):
            moved = parts[g] - parts[g][:, j : j + 1] * scaled
            if g == home:
                if full:
                    moved = jnp.where(sub == at, scaled, moved)
                else:
                    moved = jnp.where(sub > at, moved, parts[g])
            parts[g] = moved
    return jnp.concatenate(parts, axis=0)


def factor_into(gram, r_ref, linv_ref, work):
    work[:, :B] = gram
    work[:, B:] = eye(B)
    for o in range(0, B, NB):
        whole = jnp.concatenate([work[o : o + NB, o : o + NB], eye(NB)], axis=1)
        done = eliminate_some(whole, range(NB), False)
        diag = jnp.sum(done[:, :NB] * eye(NB), axis=1, keepdims=True)
        scaled = done[:, NB:] * lax.rsqrt(diag)
        strip = contract(scaled, work[o : o + NB, :], 1, 0)
        rows = o + lax.broadcasted_iota(jnp.int32, (NB, B), 0)
        cols = lax.broadcasted_iota(jnp.int32, (NB, B), 1)
        r_ref[o : o + NB, :] = jnp.where(cols >= rows, strip[:, :B], 0.0)
        linv_ref[o : o + NB, :] = strip[:, B:]
        if o + NB < B:
            below = contract(strip[:, :B], strip, 0, 0)
            work[o + NB :, :] = work[o + NB :, :] - below[o + NB :, :]


def update_kernel(scale, a_ref, p_ref, u_ref, x1_ref, y_ref, x_ref, r_ref, o_ref, right):
    step = pl.program_id(0)
    row_at = lax.axis_index("row")
    col_at = lax.axis_index("col")
    cols_dev = a_ref.shape[1]

    @pl.when(step == 0)
    def _():
        for at, ref in ((0, x1_ref), (3, y_ref)):
            high, low = split(ref[...])
            right[at * B : (at + 1) * B, :] = high
            right[(at + 1) * B : (at + 2) * B, :] = high
            right[(at + 2) * B : (at + 3) * B, :] = low

    p_high, p_low = split(p_ref[...])
    u_high, u_low = split(u_ref[...])
    left = jnp.concatenate([p_high, p_low, p_high, u_high, u_low, u_high], axis=1)
    o_ref[...] = a_ref[...] - jnp.dot(left, right[...], preferred_element_type=jnp.float32)

    first = jnp.logical_and(step == 0, row_at == 0)

    @pl.when(first)
    def _():
        o_ref[B : 2 * B, :] = o_ref[B : 2 * B, :] + x_ref[...]
        global_cols = col_at * cols_dev + lax.broadcasted_iota(jnp.int32, (B, cols_dev), 1)
        band = lax.broadcasted_iota(jnp.int32, (B, cols_dev), 0)
        onehot = (global_cols - B == band).astype(jnp.float32)
        mirror = contract(r_ref[...] * scale, onehot, 0, 0)
        o_ref[:B, :] = jnp.where(global_cols >= B, mirror, o_ref[:B, :])

    @pl.when(jnp.logical_and(first, col_at == 0))
    def _():
        o_ref[B : 2 * B, :B] = r_ref[...] * scale

    @pl.when(jnp.logical_and(jnp.logical_not(first), col_at == 0))
    def _():
        o_ref[:, :B] = jnp.zeros((TILE, B), jnp.float32)


def update(current, panel, u_rows, x1, y, x, r_mat, order):
    rows_dev, cols_dev = current.shape
    tall = pl.BlockSpec((TILE, B), lambda i: (i, 0))
    flat = pl.BlockSpec((B, cols_dev), lambda i: (0, 0))
    wide = pl.BlockSpec((TILE, cols_dev), lambda i: (i, 0))
    scale = 1.0 / math.sqrt(order)

    def kernel(*refs):
        update_kernel(scale, *refs)

    return pl.pallas_call(
        kernel,
        grid=(rows_dev // TILE,),
        out_shape=jax.ShapeDtypeStruct((rows_dev, cols_dev), jnp.float32),
        in_specs=[wide, tall, tall, flat, flat, flat, pl.BlockSpec((B, B), lambda i: (0, 0))],
        out_specs=wide,
        scratch_shapes=[pltpu.VMEM((6 * B, cols_dev), jnp.bfloat16)],
        compiler_params=pltpu.CompilerParams(vmem_limit_bytes=48 * 1024 * 1024),
    )(current, panel, u_rows, x1, y, x, r_mat)


def ring_of(mesh):
    coords = [tuple(d.coords) for d in mesh.devices[0][::2]]
    moving = [i for i in range(3) if len({c[i] for c in coords}) > 1]
    index = {c: i for i, c in enumerate(coords)}
    long_axis, short_axis = moving[0], moving[-1]
    tall = sorted({c[long_axis] for c in coords})
    flat = sorted({c[short_axis] for c in coords})

    def chip(a, b):
        at = list(coords[0])
        at[long_axis], at[short_axis] = tall[a], flat[b]
        return index[tuple(at)]

    order = [chip(a, 0) for a in range(len(tall) - 1, -1, -1)]
    for a in range(len(tall)):
        across = range(1, len(flat)) if a % 2 == 0 else range(len(flat) - 1, 0, -1)
        order += [chip(a, b) for b in across]
    return order


def look_up(table, at):
    found = jnp.int32(table[0])
    for i in range(1, len(table)):
        found = jnp.where(at == i, jnp.int32(table[i]), found)
    return found


def ring_gather(ring, n_row, out_ref, first_ref, sems):
    ring_send, ring_recv, sib_send, sib_recv = sems
    row_at, col_at = lax.axis_index("row"), lax.axis_index("col")
    n = len(ring)
    rows = first_ref.shape[0]
    cut = rows // SUB
    chip, core = col_at // 2, lax.rem(col_at, 2)
    per_plane = n // n_row
    place = look_up([ring.index(i) for i in range(n)], chip)
    way = 1 - 2 * core
    next_col = 2 * look_up(ring, lax.rem(place + way + n, n)) + core
    prev_col = 2 * look_up(ring, lax.rem(place - way + n, n)) + core
    sib_col = 2 * chip + 1 - core

    barrier = pltpu.get_barrier_semaphore()
    for col in (next_col, prev_col, sib_col):
        pl.semaphore_signal(barrier, inc=1, device_id=(row_at, col), device_id_type=MESH)
    for other in peers(n_row, row_at):
        pl.semaphore_signal(barrier, inc=1, device_id=(other, col_at), device_id_type=MESH)
    pl.semaphore_wait(barrier, 3 + n_row - 1)

    def start_of(source, of_core):
        return pl.multiple_of((source * 2 + of_core) * rows, 8)

    def window(source, of_core, sub):
        return out_ref.at[pl.ds(pl.multiple_of(start_of(source, of_core) + sub * cut, 8), cut)]

    def ring_copy(source, sub, src):
        return pltpu.make_async_remote_copy(
            src_ref=src,
            dst_ref=window(source, core, sub),
            send_sem=ring_send.at[source, sub],
            recv_sem=ring_recv.at[source, sub],
            device_id=(row_at, next_col),
            device_id_type=MESH,
        )

    def sib_copy(source, of_core, sub, src):
        return pltpu.make_async_remote_copy(
            src_ref=src,
            dst_ref=window(source, of_core, sub),
            send_sem=sib_send.at[source, sub],
            recv_sem=sib_recv.at[source, sub],
            device_id=(row_at, sib_col),
            device_id_type=MESH,
        )

    def found(step, turn):
        at = look_up(ring, lax.rem(place - turn * step + n, n))
        source = at - row_at * per_plane
        valid = jnp.logical_and(source >= 0, source < per_plane)
        return valid, jnp.clip(source, 0, per_plane - 1)

    has_home, home = found(0, way)

    def begin(sub, src_ref):
        src = src_ref.at[pl.ds(sub * cut, cut)]
        ring_copy(home, sub, src).start()
        sib_copy(home, core, sub, src).start()

    def keep(src_ref):
        out_ref[pl.ds(start_of(home, core), rows), :] = src_ref[...]

    def forward(step, sub):
        valid, source = found(step, way)

        @pl.when(valid)
        def _():
            src = window(source, core, sub)
            ring_copy(source, sub, src).wait_recv()

            @pl.when(step < n - 1)
            def _():
                ring_copy(source, sub, src).start()

            sib_copy(source, core, sub, src).start()

    def from_sibling(source):
        for sub in range(SUB):
            sib_copy(source, 1 - core, sub, window(source, core, sub)).wait_recv()

    def finish():
        def sent(step, carry):
            valid, source = found(step, way)

            @pl.when(valid)
            def _():
                for sub in range(SUB):
                    src = window(source, core, sub)

                    @pl.when(step < n - 1)
                    def _():
                        ring_copy(source, sub, src).wait_send()

                    sib_copy(source, core, sub, src).wait_send()

            return carry

        lax.fori_loop(0, n, sent, 0)

    return dict(
        n=n, way=way, core=core, has_home=has_home, start_of=start_of, found=found, begin=begin, keep=keep,
        forward=forward, from_sibling=from_sibling, finish=finish,
    )


def split(value):
    high = value.astype(jnp.bfloat16)
    low = (value - high.astype(jnp.float32)).astype(jnp.bfloat16)
    return high, low


def product(left_op, right_op):
    left_high, left_low = split(left_op)
    right_high, right_low = split(right_op)
    left = jnp.concatenate([left_high, left_low, left_high], axis=0)
    right = jnp.concatenate([right_high, right_high, right_low], axis=0)
    return lax.dot_general(
        left, right, (((0,), (0,)), ((), ())), preferred_element_type=jnp.float32
    )


def panel_kernel(
    ring, n_row, first_ref, extra_ref, a_ref, out_ref, chunk_ref, beside_ref, k_ref, gram_ref,
    held, a_sem, ring_send, ring_recv, sib_send, sib_recv, hop_send, hop_recv, beside_send, beside_recv,
):
    row_at, col_at = lax.axis_index("row"), lax.axis_index("col")
    rows = first_ref.shape[0]
    cut = rows // SUB
    load = pltpu.make_async_copy(a_ref, held, a_sem)
    load.start()
    g = ring_gather(ring, n_row, out_ref, first_ref, (ring_send, ring_recv, sib_send, sib_recv))
    has_home = g["has_home"]

    def hop_copy(other, sub):
        return pltpu.make_async_remote_copy(
            src_ref=first_ref.at[pl.ds(sub * cut, cut)],
            dst_ref=chunk_ref.at[pl.ds(sub * cut, cut)],
            send_sem=hop_send.at[other - 1, sub],
            recv_sem=hop_recv.at[sub],
            device_id=(other, col_at),
            device_id_type=MESH,
        )

    def beside_copy(other):
        return pltpu.make_async_remote_copy(
            src_ref=extra_ref,
            dst_ref=beside_ref,
            send_sem=beside_send.at[other - 1],
            recv_sem=beside_recv,
            device_id=(other, col_at),
            device_id_type=MESH,
        )

    @pl.when(row_at == 0)
    def _():
        for sub in range(SUB):
            @pl.when(has_home)
            def _():
                g["begin"](sub, first_ref)

            for other in range(1, n_row):
                hop_copy(other, sub).start()
        for other in range(1, n_row):
            beside_copy(other).start()
        chunk_ref[...] = first_ref[...]
        beside_ref[...] = extra_ref[...]

        @pl.when(has_home)
        def _():
            g["keep"](first_ref)

    @pl.when(jnp.logical_and(row_at > 0, has_home))
    def _():
        for sub in range(SUB):
            hop_copy(1, sub).wait_recv()
            g["begin"](sub, chunk_ref)
        g["keep"](chunk_ref)

    k_ref[...] = jnp.zeros_like(k_ref)
    gram_ref[...] = jnp.zeros_like(gram_ref)
    load.wait()

    def absorb(source, of_core):
        at = pl.ds(g["start_of"](source, of_core), rows)
        panel = out_ref[at, :]
        k_ref[...] += product(panel, held[at, :])
        gram_ref[...] += contract(panel, panel, 0, 0)

    def step_on(step, carry):
        valid, source = g["found"](step, g["way"])

        @pl.when(step > 0)
        def _():
            for sub in range(SUB):
                g["forward"](step, sub)

        @pl.when(valid)
        def _():
            absorb(source, g["core"])

        sib_valid, sib_source = g["found"](step, -g["way"])

        @pl.when(sib_valid)
        def _():
            g["from_sibling"](sib_source)
            absorb(sib_source, 1 - g["core"])

        return carry

    lax.fori_loop(0, g["n"], step_on, 0)
    g["finish"]()

    @pl.when(row_at == 0)
    def _():
        for other in range(1, n_row):
            for sub in range(SUB):
                hop_copy(other, sub).wait_send()
            beside_copy(other).wait_send()

    @pl.when(row_at > 0)
    def _():
        beside_copy(1).wait_recv()

    @pl.when(jnp.logical_and(row_at > 0, jnp.logical_not(has_home)))
    def _():
        for sub in range(SUB):
            hop_copy(1, sub).wait_recv()


def panel_terms(first, extra, symmetric, ring, n_row):
    per_plane = len(ring) // n_row
    dma = pltpu.SemaphoreType.DMA
    rows = first.shape[0]

    def kernel(*refs):
        panel_kernel(ring, n_row, *refs)

    def shape(*dims):
        return jax.ShapeDtypeStruct(dims, jnp.float32)

    return pl.pallas_call(
        kernel,
        out_shape=(
            shape(symmetric.shape[0], B), shape(rows, B), shape(rows, B), shape(B, rows), shape(B, B)
        ),
        in_specs=[VMEM, VMEM, pl.BlockSpec(memory_space=pl.ANY)],
        out_specs=(VMEM,) * 5,
        scratch_shapes=[pltpu.VMEM(symmetric.shape, jnp.float32), dma]
        + [dma((per_plane, SUB))] * 4
        + [dma((n_row - 1, SUB)), dma((SUB,)), dma((n_row - 1,)), dma],
        compiler_params=pltpu.CompilerParams(
            collective_id=1, has_side_effects=True, vmem_limit_bytes=56 * 1024 * 1024
        ),
    )(first, extra, symmetric)


def inverse_tasks(lead_ref, linv_ref, t_ref, work, block):
    tasks = []

    def begin():
        work[:, :B] = eye(B) - contract(lead_ref[...], linv_ref[...], 1, 1)
        work[:, B:] = eye(B)

    tasks.append(begin)
    for o in range(0, B, NB):
        def load(o=o):
            block[...] = jnp.concatenate([work[o : o + NB, o : o + NB], eye(NB)], axis=1)

        tasks.append(load)
        for j in range(0, NB, 4):
            def some(j=j):
                block[...] = eliminate_some(block[...], range(j, j + 4), True)

            tasks.append(some)

        def spread(o=o):
            strip = contract(block[:, NB:], work[o : o + NB, :], 1, 0)
            change = contract(work[:, o : o + NB], strip, 1, 0)
            work[...] = work[...] - change
            work[o : o + NB, :] = strip

        tasks.append(spread)

    def end():
        t_ref[...] = work[:, B:]

    tasks.append(end)
    return tasks


def product_kernel(
    ring, n_row, u_ref, v_ref, lead_ref, linv_ref, panel_ref, out_ref, x_ref, x1_ref, y_ref,
    t_ref, work, block, z_ref, z_in, ring_send, ring_recv, sib_send, sib_recv, z_send, z_recv,
):
    row_at, col_at = lax.axis_index("row"), lax.axis_index("col")
    rows = u_ref.shape[0]
    g = ring_gather(ring, n_row, out_ref, u_ref, (ring_send, ring_recv, sib_send, sib_recv))
    has_home, n = g["has_home"], g["n"]

    @pl.when(has_home)
    def _():
        for sub in range(SUB):
            g["begin"](sub, u_ref)
        g["keep"](u_ref)

    tasks = inverse_tasks(lead_ref, linv_ref, t_ref, work, block)
    slots = (n - 1) * SUB
    done = 0
    for slot in range(slots):
        g["forward"](1 + slot // SUB, slot % SUB)
        until = (slot + 1) * len(tasks) // slots
        for task in tasks[done:until]:
            task()
        done = until
    t_mat = t_ref[...]
    y_ref[...] = contract(t_mat, v_ref[...], 0, 1)
    x_ref[...] = contract(t_mat, u_ref[...], 1, 1)
    z_ref[...] = jnp.zeros_like(z_ref)

    def absorb(source, carry):
        g["from_sibling"](source)
        at = pl.ds(pl.multiple_of(source * 2 * rows, 8), 2 * rows)
        z_ref[...] += product(panel_ref[at, :], out_ref[at, :])
        return carry

    lax.fori_loop(0, n // n_row, absorb, 0)
    own = jnp.where(row_at == 0, out_ref[B : 2 * B, :], 0.0)
    z_ref[...] = contract(linv_ref[...], z_ref[...], 1, 0) - own
    copies = exchange(n_row, row_at, col_at, z_ref, z_in, z_send, z_recv)
    g["finish"]()
    core_sum = total(n_row, z_ref, z_in, copies)
    middle = contract(contract(t_mat, core_sum, 1, 0), t_mat, 1, 1)
    x = x_ref[...] - contract(middle, v_ref[...], 1, 1)
    x_ref[...] = x
    x1_ref[...] = contract(linv_ref[...], x, 0, 0)
    for copy in copies:
        copy.wait_send()


def product_terms(u_col, v_col, lead, linv, panel, ring, n_row):
    per_plane = len(ring) // n_row
    dma = pltpu.SemaphoreType.DMA
    flat = jax.ShapeDtypeStruct(u_col.shape[::-1], jnp.float32)

    def kernel(*refs):
        product_kernel(ring, n_row, *refs)

    def scratch(*dims):
        return pltpu.VMEM(dims, jnp.float32)

    return pl.pallas_call(
        kernel,
        out_shape=(jax.ShapeDtypeStruct(panel.shape, jnp.float32), flat, flat, flat),
        in_specs=[VMEM] * 5,
        out_specs=(VMEM,) * 4,
        scratch_shapes=[
            scratch(B, B), scratch(B, 2 * B), scratch(NB, 2 * NB), scratch(B, B), scratch(n_row - 1, B, B)
        ]
        + [dma((per_plane, SUB))] * 4
        + [dma((n_row - 1,))] * 2,
        compiler_params=pltpu.CompilerParams(
            collective_id=3, has_side_effects=True, vmem_limit_bytes=56 * 1024 * 1024
        ),
    )(u_col, v_col, lead, linv, panel)


def peers(n_row, row_at):
    return [lax.rem(row_at + d, n_row) for d in range(1, n_row)]


def greet(n_row, row_at, col_at):
    barrier = pltpu.get_barrier_semaphore()
    for other in peers(n_row, row_at):
        pl.semaphore_signal(barrier, inc=1, device_id=(other, col_at), device_id_type=MESH)
    pl.semaphore_wait(barrier, n_row - 1)


def exchange(n_row, row_at, col_at, src, landing, send, recv):
    copies = []
    for at, other in enumerate(peers(n_row, row_at)):
        copy = pltpu.make_async_remote_copy(
            src_ref=src,
            dst_ref=landing.at[at],
            send_sem=send.at[at],
            recv_sem=recv.at[at],
            device_id=(other, col_at),
            device_id_type=MESH,
        )
        copy.start()
        copies.append(copy)
    return copies


def total(n_row, src, landing, copies):
    for copy in copies:
        copy.wait_recv()
    found = src[...]
    for at in range(n_row - 1):
        found = found + landing[at]
    return found


def basis_kernel(
    n_row, gram_ref, k_ref, lead_ref, p_ref, e_ref, r_ref, linv_ref, lead_out, u_ref, v_ref,
    work, gram_in, k_in, gram_send, gram_recv, k_send, k_recv, lead_send, lead_recv,
):
    row_at, col_at = lax.axis_index("row"), lax.axis_index("col")
    greet(n_row, row_at, col_at)
    gram_copies = exchange(n_row, row_at, col_at, gram_ref, gram_in, gram_send, gram_recv)

    def lead_copy(other):
        return pltpu.make_async_remote_copy(
            src_ref=lead_ref,
            dst_ref=lead_out,
            send_sem=lead_send.at[other - 1],
            recv_sem=lead_recv,
            device_id=(other, col_at),
            device_id_type=MESH,
        )

    k_copies = exchange(n_row, row_at, col_at, k_ref, k_in, k_send, k_recv)

    @pl.when(row_at == 0)
    def _():
        for other in range(1, n_row):
            lead_copy(other).start()
        lead_out[...] = lead_ref[...]

    gram = total(n_row, gram_ref, gram_in, gram_copies)
    factor_into(gram, r_ref, linv_ref, work)
    linv = linv_ref[...]
    cols_dev = p_ref.shape[0]
    global_cols = col_at * cols_dev + lax.broadcasted_iota(jnp.int32, (cols_dev, B), 0)
    band = lax.broadcasted_iota(jnp.int32, (cols_dev, B), 1)
    col_unit = (global_cols - B == band).astype(jnp.float32)
    v_ref[...] = contract(p_ref[...], linv, 1, 1) - col_unit
    q_col = total(n_row, k_ref, k_in, k_copies)
    u_ref[...] = contract(q_col, linv, 0, 1) - e_ref[...]
    for copy in gram_copies + k_copies:
        copy.wait_send()

    @pl.when(row_at == 0)
    def _():
        for other in range(1, n_row):
            lead_copy(other).wait_send()

    @pl.when(row_at > 0)
    def _():
        lead_copy(1).wait_recv()


def basis(n_row, gram, k, lead, p_col, e_col):
    dma = pltpu.SemaphoreType.DMA
    small = jax.ShapeDtypeStruct((B, B), jnp.float32)
    part = jax.ShapeDtypeStruct(p_col.shape, jnp.float32)
    others = dma((n_row - 1,))

    def kernel(*refs):
        basis_kernel(n_row, *refs)

    return pl.pallas_call(
        kernel,
        out_shape=(small, small, small, part, part),
        in_specs=[VMEM] * 5,
        out_specs=(VMEM,) * 5,
        scratch_shapes=[
            pltpu.VMEM((B, 2 * B), jnp.float32),
            pltpu.VMEM((n_row - 1, B, B), jnp.float32),
            pltpu.VMEM((n_row - 1,) + k.shape, jnp.float32),
            others, others, others, others, others, dma,
        ],
        compiler_params=pltpu.CompilerParams(
            collective_id=2, has_side_effects=True, vmem_limit_bytes=48 * 1024 * 1024
        ),
    )(gram, k, lead, p_col, e_col)


def per_device(ring, n_row, symmetric):
    cols_dev = symmetric.shape[1]
    order = symmetric.shape[0] * n_row
    global_cols = lax.axis_index("col") * cols_dev + jnp.arange(cols_dev, dtype=jnp.int32)

    strip = jnp.where((global_cols >= B)[None, :], symmetric[:B], jnp.float32(0.0))
    panel, p_col, e_col, k_part, gram_part = panel_terms(
        strip.T, symmetric[B : 2 * B].T, symmetric, ring, n_row
    )
    r_mat, linv, lead, u_col, v_col = basis(
        n_row, gram_part, k_part, panel[B : 2 * B], p_col, e_col
    )
    u_rows, x, x1, y = product_terms(u_col, v_col, lead, linv, panel, ring, n_row)
    return update(symmetric, panel, u_rows, x1, y, x, r_mat, order)


def solution(mesh):
    n_row = mesh.shape["row"]

    ring = ring_of(mesh)

    def run(symmetric):
        return per_device(ring, n_row, symmetric)

    return jax.shard_map(
        run, mesh=mesh, in_specs=(P("row", "col"),), out_specs=P("row", "col"), check_vma=False
    )
```

time: 328 us -> 235 us (0.72); the launches traced: 322 us -> 234 us
  matrix products: 48.7 us -> 0 us
  Pallas kernels: 266 us -> 218 us
  local copies, waits for them, and re-layouts: 6.34 us -> 14.9 us
    pallas_call x4 -> x2, Pallas kernels: 203 us -> 146 us  [the longest x1 80 us: product_terms(): pl.pallas_call(kernel, out_shape=(jax.ShapeDtypeStruct(panel.shape, jnp.f...]
    dot_general x4 -> x0, matrix products: 48.7 us -> none  [contract(): lax.dot_general(left_op, right_op, (((left_dim,), (right_dim,)), ((), ())...]
    pallas_call x1, Pallas kernels: 36.5 us -> 46.3 us  [basis(): pl.pallas_call(kernel, out_shape=(small, small, small, part, part), in_sp...]
    unnamed x22 -> x24, local copies, waits for them, and re-layouts: 3.75 us -> 12.4 us
where the time goes in v3:
time: 235 us; the launch traced here: 234 us
  Pallas kernels  218 us (93%)
  local copies, waits for them, and re-layouts  14.9 us (6%)
    pallas_call x1, Pallas kernels, product_terms(): pl.pallas_call(kernel, out_shape=(jax.ShapeDtypeStruct(panel.shape, jnp.f...  80 us
    pallas_call x1, Pallas kernels, panel_terms(): pl.pallas_call(kernel, out_shape=(shape(symmetric.shape[0], B), shape(row...  65.7 us
    pallas_call x1, Pallas kernels, basis(): pl.pallas_call(kernel, out_shape=(small, small, small, part, part), in_sp...  46.3 us
    pallas_call x1, Pallas kernels, update(): pl.pallas_call(kernel, grid=(rows_dev // TILE,), out_shape=jax.ShapeDtype...  26.1 us
    unnamed x24, local copies, waits for them, and re-layouts  12.4 us

profile of v3, /device:TPU:0, one launch (start us, length us, event | category | flops | bytes accessed | tf_op | source)
XLA Modules:
  0.0 234.1 jit_solution(5101520930489616593)
XLA Ops:
  0.0 1.5 fusion
  1.5 1.2 copy.5
  2.7 0.3 copy.4
  2.9 1.1 select_bitcast_fusion.refs_0_
  4.0 65.7 %shard_map.17 = (f32[6144,256]{1,0:T(8,128)}, f32[768,256]{1,0:T(8,128)}, f32[768,256]{1,0:T(8,128)}, f32[256,768]{1,0:T(8,128)}, f32[256,256]{1,0:T(8,128)}) custom-call(f32[768,256]{1,0:T(8,128)} %select_bitcast_fusion.refs_0_, f32[768,256]{1,0:T(8,128)} %bitcast.3, f32[6144,768]{1,0:T(8,128)} %refs_0_.1), custom_call_target="tpu_custom_call" | custom-call | tf_op jit(solution)/shard_map/pallas_call | solution.py:400
  69.7 1.0 slice.11.refs_2_
  70.7 0.0 copy-start.2
  70.7 1.1 copy-done.2
  71.8 0.0 copy-start.3
  71.8 1.1 copy-done.3
  73.0 0.0 copy-start.4
  73.0 1.1 copy-done.4
  74.1 0.0 copy-start.10
  74.1 0.9 copy-done.10
  75.0 46.3 %shard_map.18 = (f32[256,256]{1,0:T(8,128)S(1)}, f32[256,256]{1,0:T(8,128)S(1)}, f32[256,256]{1,0:T(8,128)S(1)}, f32[768,256]{1,0:T(8,128)S(1)}, f32[768,256]{1,0:T(8,128)S(1)}) custom-call(f32[256,256]{1,0:T(8,128)S(1)} %copy-done.10, f32[256,768]{1,0:T(8,128)S(1)} %copy-done.4, f32[256,256]{1,0:T(8,128)S(1)} %slice.11.refs_2_, f32[768,256]{1,0:T(8,128)S(1)} %copy-done.2, ...), custom_call_target="tpu_custom_call" | custom-call | tf_op jit(solution)/shard_map/pallas_call | solution.py:620
  121.3 0.0 copy-start
  121.4 0.9 copy-done
  122.2 0.0 copy-start.1
  122.2 1.0 copy-done.1
  123.2 0.0 copy-start.8
  123.2 0.7 copy-done.8
  123.9 0.0 copy-start.9
  123.9 0.7 copy-done.9
  124.6 80.0 %shard_map.19 = (f32[6144,256]{1,0:T(8,128)}, f32[256,768]{1,0:T(8,128)}, f32[256,768]{1,0:T(8,128)}, f32[256,768]{1,0:T(8,128)}) custom-call(f32[768,256]{1,0:T(8,128)} %copy-done, f32[768,256]{1,0:T(8,128)} %copy-done.1, f32[256,256]{1,0:T(8,128)} %copy-done.9, f32[256,256]{1,0:T(8,128)} %copy-done.8, f32[6144,256]{1,0:T(8,128)} %get-tuple-element.19.refs_4_.refs_1_), custom_call_target="tpu_custom_call" | custom-call | tf_op jit(solution)/shard_map/pallas_call | solution.py:510
  204.6 0.0 copy-start.5
  204.6 1.1 copy-done.5
  205.7 0.0 copy-start.6
  205.7 1.1 copy-done.6
  206.8 0.0 copy-start.7
  206.8 1.1 copy-done.7
  208.0 26.1 %shard_map.20 = f32[6144,768]{1,0:T(8,128)} custom-call(f32[6144,768]{1,0:T(8,128)} %refs_0_.1, f32[6144,256]{1,0:T(8,128)} %get-tuple-element.19.refs_4_.refs_1_, f32[6144,256]{1,0:T(8,128)} %get-tuple-element.28.refs_2_, f32[256,768]{1,0:T(8,128)S(1)} %copy-done.6, f32[256,768]{1,0:T(8,128)S(1)} %copy-done.7, f32[256,768]{1,0:T(8,128)S(1)} %copy-done.5, ...), custom_call_target="tpu_custom_call" | custom-call | tf_op jit(solution)/shard_map/pallas_call | solution.py:121
  (1 shorter events, 0.0 us)
Async XLA Ops:
  70.7 1.1 copy-start.2
  71.8 1.1 copy-start.3
  73.0 1.1 copy-start.4
  74.1 0.9 copy-start.10
  121.3 0.9 copy-start
  122.2 1.0 copy-start.1
  123.2 0.7 copy-start.8
  123.9 0.7 copy-start.9
  204.6 1.1 copy-start.5
  205.7 1.1 copy-start.6
  206.8 1.1 copy-start.7

commit v4 on v3

--- a/solution.py
+++ b/solution.py
@@ -9,7 +9,7 @@
 
 B = 256
 NB = 64
-TILE = 512
+TILE = 768
 SUB = 8
 MESH = pl.DeviceIdType.MESH
 HIGH = lax.Precision.HIGH
@@ -36,17 +36,27 @@
 def eliminate_some(whole, columns, full):
     parts = [whole[8 * g : 8 * g + 8] for g in range(NB // 8)]
     sub = lax.broadcasted_iota(jnp.int32, (8, 2 * NB), 0)
+    whole_tile = (8, 2 * NB)
     for j in columns:
         home, at = j // 8, j % 8
-        row = parts[home][at : at + 1, :]
-        scaled = row * (1.0 / row[:, j : j + 1])
+        top = jnp.broadcast_to(parts[home][at : at + 1, :], whole_tile)
+        low = jnp.broadcast_to(parts[home][at + 1 : at + 2, :], whole_tile)
+        top_0 = jnp.broadcast_to(top[:, j : j + 1], whole_tile)
+        top_1 = jnp.broadcast_to(top[:, j + 1 : j + 2], whole_tile)
+        low_0 = jnp.broadcast_to(low[:, j : j + 1], whole_tile)
+        low_1 = jnp.broadcast_to(low[:, j + 1 : j + 2], whole_tile)
+        over = 1.0 / top_0
+        ratio = low_0 * over
+        second = low - ratio * top
+        row_1 = second * (1.0 / (low_1 - ratio * top_1))
+        row_0 = top * over - (top_1 * over) * row_1
         for g in range(0 if full else home, NB // 8):
-            moved = parts[g] - parts[g][:, j : j + 1] * scaled
+            moved = parts[g] - parts[g][:, j : j + 1] * row_0 - parts[g][:, j + 1 : j + 2] * row_1
             if g == home:
                 if full:
-                    moved = jnp.where(sub == at, scaled, moved)
+                    moved = jnp.where(sub == at, row_0, jnp.where(sub == at + 1, row_1, moved))
                 else:
-                    moved = jnp.where(sub > at, moved, parts[g])
+                    moved = jnp.where(sub > at + 1, moved, jnp.where(sub == at + 1, second, parts[g]))
             parts[g] = moved
     return jnp.concatenate(parts, axis=0)
 
@@ -56,7 +66,7 @@
     work[:, B:] = eye(B)
     for o in range(0, B, NB):
         whole = jnp.concatenate([work[o : o + NB, o : o + NB], eye(NB)], axis=1)
-        done = eliminate_some(whole, range(NB), False)
+        done = eliminate_some(whole, range(0, NB, 2), False)
         diag = jnp.sum(done[:, :NB] * eye(NB), axis=1, keepdims=True)
         scaled = done[:, NB:] * lax.rsqrt(diag)
         strip = contract(scaled, work[o : o + NB, :], 1, 0)
@@ -279,7 +289,7 @@
 
 
 def panel_kernel(
-    ring, n_row, first_ref, extra_ref, a_ref, out_ref, chunk_ref, beside_ref, k_ref, gram_ref,
+    ring, n_row, first_ref, extra_ref, a_ref, out_ref, chunk_ref, beside_ref, k_ref, gram_ref, lead_ref,
     held, a_sem, ring_send, ring_recv, sib_send, sib_recv, hop_send, hop_recv, beside_send, beside_recv,
 ):
     row_at, col_at = lax.axis_index("row"), lax.axis_index("col")
@@ -339,34 +349,44 @@
     gram_ref[...] = jnp.zeros_like(gram_ref)
     load.wait()
 
-    def absorb(source, of_core):
-        at = pl.ds(g["start_of"](source, of_core), rows)
+    part = rows // 2
+
+    def absorb(source, of_core, half):
+        start = g["start_of"](source, of_core) + half * part
+        at = pl.ds(pl.multiple_of(start, 8), part)
         panel = out_ref[at, :]
         k_ref[...] += product(panel, held[at, :])
         gram_ref[...] += contract(panel, panel, 0, 0)
 
-    def step_on(step, carry):
+    def own_part(step, half):
         valid, source = g["found"](step, g["way"])
-
-        @pl.when(step > 0)
-        def _():
-            for sub in range(SUB):
-                g["forward"](step, sub)
 
         @pl.when(valid)
         def _():
-            absorb(source, g["core"])
-
-        sib_valid, sib_source = g["found"](step, -g["way"])
-
-        @pl.when(sib_valid)
+            absorb(source, g["core"], half)
+
+    def sibling_part(step, half):
+        valid, source = g["found"](step, -g["way"])
+
+        @pl.when(valid)
         def _():
-            g["from_sibling"](sib_source)
-            absorb(sib_source, 1 - g["core"])
-
+            if half == 0:
+                g["from_sibling"](source)
+            absorb(source, 1 - g["core"], half)
+
+    works = [(own_part, 0), (own_part, 1), (sibling_part, 0), (sibling_part, 1)]
+
+    def step_on(step, carry):
+        for at, (work, half) in enumerate(works):
+            for sub in range(at * SUB // 4, (at + 1) * SUB // 4):
+                g["forward"](step, sub)
+            work(step - 1, half)
         return carry
 
-    lax.fori_loop(0, g["n"], step_on, 0)
+    lax.fori_loop(1, g["n"], step_on, 0)
+    for work, half in works:
+        work(g["n"] - 1, half)
+    lead_ref[...] = out_ref[B : 2 * B, :]
     g["finish"]()
 
     @pl.when(row_at == 0)
@@ -400,10 +420,11 @@
     return pl.pallas_call(
         kernel,
         out_shape=(
-            shape(symmetric.shape[0], B), shape(rows, B), shape(rows, B), shape(B, rows), shape(B, B)
+            shape(symmetric.shape[0], B), shape(rows, B), shape(rows, B), shape(B, rows), shape(B, B),
+            shape(B, B),
         ),
         in_specs=[VMEM, VMEM, pl.BlockSpec(memory_space=pl.ANY)],
-        out_specs=(VMEM,) * 5,
+        out_specs=(VMEM,) * 6,
         scratch_shapes=[pltpu.VMEM(symmetric.shape, jnp.float32), dma]
         + [dma((per_plane, SUB))] * 4
         + [dma((n_row - 1, SUB)), dma((SUB,)), dma((n_row - 1,)), dma],
@@ -428,7 +449,7 @@
         tasks.append(load)
         for j in range(0, NB, 4):
             def some(j=j):
-                block[...] = eliminate_some(block[...], range(j, j + 4), True)
+                block[...] = eliminate_some(block[...], range(j, j + 4, 2), True)
 
             tasks.append(some)
 
@@ -640,11 +661,11 @@
     global_cols = lax.axis_index("col") * cols_dev + jnp.arange(cols_dev, dtype=jnp.int32)
 
     strip = jnp.where((global_cols >= B)[None, :], symmetric[:B], jnp.float32(0.0))
-    panel, p_col, e_col, k_part, gram_part = panel_terms(
+    panel, p_col, e_col, k_part, gram_part, lead_part = panel_terms(
         strip.T, symmetric[B : 2 * B].T, symmetric, ring, n_row
     )
     r_mat, linv, lead, u_col, v_col = basis(
-        n_row, gram_part, k_part, panel[B : 2 * B], p_col, e_col
+        n_row, gram_part, k_part, lead_part, p_col, e_col
     )
     u_rows, x, x1, y = product_terms(u_col, v_col, lead, linv, panel, ring, n_row)
     return update(symmetric, panel, u_rows, x1, y, x, r_mat, order)

time: 235 us -> 221 us (0.940)
  Pallas kernels: 218 us -> 205 us
    pallas_call x1, Pallas kernels: 46.3 us -> 41.3 us  [basis(): pl.pallas_call(kernel, out_shape=(small, small, small, part, part), in_sp...]
    pallas_call x1, Pallas kernels: 80 us -> 76.3 us  [product_terms(): pl.pallas_call(kernel, out_shape=(jax.ShapeDtypeStruct(panel.shape, jnp.f...]
    pallas_call x1, Pallas kernels: 65.7 us -> 62.5 us  [panel_terms(): pl.pallas_call(kernel, out_shape=(shape(symmetric.shape[0], B), shape(row...]
    unnamed x24 -> x26, local copies, waits for them, and re-layouts: 12.4 us -> 13.4 us
where the time goes in v4:
time: 221 us
  Pallas kernels  205 us (93%)
  local copies, waits for them, and re-layouts  14.8 us (7%)
    pallas_call x1, Pallas kernels, product_terms(): pl.pallas_call(kernel, out_shape=(jax.ShapeDtypeStruct(panel.shape, jnp.f...  76.3 us
    pallas_call x1, Pallas kernels, panel_terms(): pl.pallas_call(kernel, out_shape=(shape(symmetric.shape[0], B), shape(row...  62.5 us
    pallas_call x1, Pallas kernels, basis(): pl.pallas_call(kernel, out_shape=(small, small, small, part, part), in_sp...  41.3 us
    pallas_call x1, Pallas kernels, update(): pl.pallas_call(kernel, grid=(rows_dev // TILE,), out_shape=jax.ShapeDtype...  24.4 us
    unnamed x26, local copies, waits for them, and re-layouts  13.4 us

profile of v4, /device:TPU:0, one launch (start us, length us, event | category | flops | bytes accessed | tf_op | source)
XLA Modules:
  0.0 220.5 jit_solution(924849585937290725)
XLA Ops:
  0.0 1.5 fusion
  1.5 1.2 copy.5
  2.7 0.3 copy.4
  2.9 1.1 select_bitcast_fusion.refs_0_
  4.0 62.5 %shard_map.17 = (f32[6144,256]{1,0:T(8,128)}, f32[768,256]{1,0:T(8,128)}, f32[768,256]{1,0:T(8,128)}, f32[256,768]{1,0:T(8,128)}, f32[256,256]{1,0:T(8,128)}, /*index=5*/f32[256,256]{1,0:T(8,128)}) custom-call(f32[768,256]{1,0:T(8,128)} %select_bitcast_fusion.refs_0_, f32[768,256]{1,0:T(8,128)} %bitcast.3, f32[6144,768]{1,0:T(8,128)} %refs_0_.1), custom_call_target="tpu_custom_call" | custom-call | tf_op jit(solution)/shard_map/pallas_call | solution.py:420
  66.5 0.0 copy-start.2
  66.5 1.1 copy-done.2
  67.7 0.0 copy-start.3
  67.7 1.1 copy-done.3
  68.8 0.0 copy-start.4
  68.8 1.1 copy-done.4
  69.9 0.0 copy-start.10
  69.9 0.9 copy-done.10
  70.9 0.0 copy-start.11
  70.9 0.9 copy-done.11
  71.8 41.3 %shard_map.18 = (f32[256,256]{1,0:T(8,128)S(1)}, f32[256,256]{1,0:T(8,128)S(1)}, f32[256,256]{1,0:T(8,128)S(1)}, f32[768,256]{1,0:T(8,128)S(1)}, f32[768,256]{1,0:T(8,128)S(1)}) custom-call(f32[256,256]{1,0:T(8,128)S(1)} %copy-done.10, f32[256,768]{1,0:T(8,128)S(1)} %copy-done.4, f32[256,256]{1,0:T(8,128)S(1)} %copy-done.11, f32[768,256]{1,0:T(8,128)S(1)} %copy-done.2, ...), custom_call_target="tpu_custom_call" | custom-call | tf_op jit(solution)/shard_map/pallas_call | solution.py:641
  113.2 0.0 copy-start
  113.2 0.9 copy-done
  114.0 0.0 copy-start.1
  114.0 1.0 copy-done.1
  115.0 0.0 copy-start.8
  115.0 0.7 copy-done.8
  115.7 0.0 copy-start.9
  115.7 0.7 copy-done.9
  116.4 76.3 %shard_map.19 = (f32[6144,256]{1,0:T(8,128)}, f32[256,768]{1,0:T(8,128)}, f32[256,768]{1,0:T(8,128)}, f32[256,768]{1,0:T(8,128)}) custom-call(f32[768,256]{1,0:T(8,128)} %copy-done, f32[768,256]{1,0:T(8,128)} %copy-done.1, f32[256,256]{1,0:T(8,128)} %copy-done.9, f32[256,256]{1,0:T(8,128)} %copy-done.8, f32[6144,256]{1,0:T(8,128)} %get-tuple-element.20.refs_4_.refs_1_), custom_call_target="tpu_custom_call" | custom-call | tf_op jit(solution)/shard_map/pallas_call | solution.py:531
  192.8 0.0 copy-start.5
  192.8 1.1 copy-done.5
  193.9 0.0 copy-start.6
  193.9 1.1 copy-done.6
  195.0 0.0 copy-start.7
  195.0 1.1 copy-done.7
  196.2 24.4 %shard_map.20 = f32[6144,768]{1,0:T(8,128)} custom-call(f32[6144,768]{1,0:T(8,128)} %refs_0_.1, f32[6144,256]{1,0:T(8,128)} %get-tuple-element.20.refs_4_.refs_1_, f32[6144,256]{1,0:T(8,128)} %get-tuple-element.30.refs_2_, f32[256,768]{1,0:T(8,128)S(1)} %copy-done.6, f32[256,768]{1,0:T(8,128)S(1)} %copy-done.7, f32[256,768]{1,0:T(8,128)S(1)} %copy-done.5, ...), custom_call_target="tpu_custom_call" | custom-call | tf_op jit(solution)/shard_map/pallas_call | solution.py:131
  (1 shorter events, 0.0 us)
Async XLA Ops:
  66.5 1.1 copy-start.2
  67.7 1.1 copy-start.3
  68.8 1.1 copy-start.4
  69.9 0.9 copy-start.10
  70.9 0.9 copy-start.11
  113.2 0.9 copy-start
  114.0 1.0 copy-start.1
  115.0 0.7 copy-start.8
  115.7 0.7 copy-start.9
  192.8 1.1 copy-start.5
  193.9 1.1 copy-start.6
  195.0 1.1 copy-start.7
